TPU v7x, 32 devices: a whole 2x2x4 slice. The times are simulated.
32 devices in a mesh: fsdp: 4 (over x, core), ctx: 2 (over y), tp: 4 (over z).
Axes of the slice: x: 2, y: 2, z: 4, core: 2. Of those that a mesh axis runs over, the one named last changes fastest.
Arguments:
- stream: bfloat16 [4, 1024, 2048], P('fsdp', 'ctx'), may hold values from -6 to 6
- cotangent: bfloat16 [4, 1024, 2048], P('fsdp', 'ctx'), may hold values from -6 to 6
- lengths: int32 [4], P('fsdp'), may hold values from 512 to 1024, as said below
- first_gain: bfloat16 [2048], P('fsdp'), may hold values from 0.25 to 1.75
- first_shift: bfloat16 [2048], P('fsdp'), may hold values from -3 to 3
- query_weight: bfloat16 [2048, 2048], P('fsdp', 'tp'), may hold values from -0.125 to 0.125
- query_bias: bfloat16 [16, 128], P('tp', 'fsdp'), may hold values from -3 to 3
- pair_weight: bfloat16 [2048, 256], P('fsdp'), may hold values from -0.125 to 0.125
- value_bias: bfloat16 [128], P('fsdp'), may hold values from -0.3125 to 0.3125
- output_weight: bfloat16 [2048, 2048], P('tp', 'fsdp'), may hold values from -1 to 1
- output_bias: bfloat16 [2048], P('fsdp'), may hold values from -1.75 to 1.75
- second_gain: bfloat16 [2048], P('fsdp'), may hold values from 0.25 to 1.75
- second_shift: bfloat16 [2048], P('fsdp'), may hold values from -3 to 3
- up_weight: bfloat16 [2048, 8192], P('fsdp', 'tp'), may hold values from -0.20992233 to 0.20992233
- up_bias: bfloat16 [64, 128], P('tp', 'fsdp'), may hold values from -3 to 3
- down_weight: bfloat16 [8192, 2048], P('tp', 'fsdp'), may hold values from -0.0625 to 0.0625
- down_bias: bfloat16 [2048], P('fsdp'), may hold values from -1.75 to 1.75
Outputs:
- result: bfloat16 [4, 1024, 2048], P('fsdp', 'ctx')
- stream_grad: bfloat16 [4, 1024, 2048], P('fsdp', 'ctx')
- first_gain_grad: float32 [2048], P('fsdp')
- first_shift_grad: float32 [2048], P('fsdp')
- query_weight_grad: float32 [2048, 2048], P('fsdp', 'tp')
- query_bias_grad: float32 [16, 128], P('tp', 'fsdp')
- pair_weight_grad: float32 [2048, 256], P('fsdp')
- value_bias_grad: float32 [128], P('fsdp')
- output_weight_grad: float32 [2048, 2048], P('tp', 'fsdp')
- output_bias_grad: float32 [2048], P('fsdp')
- second_gain_grad: float32 [2048], P('fsdp')
- second_shift_grad: float32 [2048], P('fsdp')
- up_weight_grad: float32 [2048, 8192], P('fsdp', 'tp')
- up_bias_grad: float32 [64, 128], P('tp', 'fsdp')
- down_weight_grad: float32 [8192, 2048], P('tp', 'fsdp')
- down_bias_grad: float32 [2048], P('fsdp')
- root_means: float32 [3], replicated
Inputs may be any that keep to these rules, and one draw needn't show every extreme that they name: `lengths`: the number of valid leading slots of each sequence; some sequence is full and some is half full.
All inputs are finite; a program needn't handle non-finite values.
Results may differ from a plain program's by a relative error of at most 0.013.
Values may be sent and summed in bfloat16 or wider, within the bound.
A program may use at most 192 MiB of HBM per device.

v0:
```python
import math

import jax
import jax.numpy as jnp
from jax import lax
from jax.sharding import PartitionSpec as P

HD = 128


EPSILON = 1e-05
NEGATIVE = -1e30


def norm_forward(inputs, norm_gain, norm_shift):
    center = inputs - jnp.mean(inputs, -1, keepdims=True)
    spread = jnp.mean(center * center, -1, keepdims=True)
    scaled = lax.rsqrt(spread + EPSILON)
    unit_rows = center * scaled
    return (unit_rows * norm_gain + norm_shift, unit_rows, scaled)


def norm_backward(upstream, unit_rows, scaled, norm_gain):
    gained = upstream * norm_gain
    return scaled * (
        gained
        - jnp.mean(gained, -1, keepdims=True)
        - unit_rows * jnp.mean(gained * unit_rows, -1, keepdims=True)
    )


def score_block(query_block, key_rows, length, query_places):
    raw_scores = jnp.einsum("qd,kd->qk", query_block, key_rows, preferred_element_type=jnp.float32)
    key_places = jnp.arange(key_rows.shape[0])
    allowed = (key_places[None, :] <= query_places[:, None]) & (key_places[None, :] < length)
    return jnp.where(allowed, raw_scores * (1.0 / math.sqrt(HD)), NEGATIVE)


def attend(query_block, pair_block, length, query_places):
    scores = score_block(query_block, pair_block[:, :HD], length, query_places)
    peak = jnp.max(scores, -1, keepdims=True)
    exponent = jnp.exp(scores - peak)
    row_total = jnp.sum(exponent, -1, keepdims=True)
    soft_weights = (exponent / row_total).astype(jnp.bfloat16)
    mixture = jnp.dot(soft_weights, pair_block[:, HD:], preferred_element_type=jnp.float32)
    return (mixture.astype(jnp.bfloat16), (peak + jnp.log(row_total))[:, 0])


def attend_back(query_block, pair_block, length, query_places, log_total, grad_mixture):
    key_rows = pair_block[:, :HD]
    value_rows = pair_block[:, HD:]
    scores = score_block(query_block, key_rows, length, query_places)
    soft_weights = jnp.exp(scores - log_total[:, None])
    grad_weights = jnp.einsum(
        "qd,kd->qk", grad_mixture, value_rows, preferred_element_type=jnp.float32
    )
    row_dot = jnp.sum(soft_weights * grad_weights, -1, keepdims=True)
    grad_scores = (soft_weights * (grad_weights - row_dot) * (1.0 / math.sqrt(HD))).astype(
        jnp.bfloat16
    )
    grad_query = jnp.dot(grad_scores, key_rows, preferred_element_type=jnp.float32)
    grad_keys = jnp.einsum(
        "qk,qd->kd", grad_scores, query_block, preferred_element_type=jnp.float32
    )
    grad_values = jnp.einsum(
        "qk,qd->kd",
        soft_weights.astype(jnp.bfloat16),
        grad_mixture,
        preferred_element_type=jnp.float32,
    )
    return (grad_query, jnp.concatenate([grad_keys, grad_values], -1))


def body(
    stream,
    cotangent,
    lengths,
    first_gain,
    first_shift,
    query_weight,
    query_bias,
    pair_weight,
    value_bias,
    output_weight,
    output_bias,
    second_gain,
    second_shift,
    up_weight,
    up_bias,
    down_weight,
    down_bias,
):
    local_weights = (
        first_gain,
        first_shift,
        query_weight,
        query_bias,
        pair_weight,
        value_bias,
        output_weight,
        output_bias,
        second_gain,
        second_shift,
        up_weight,
        up_bias,
        down_weight,
        down_bias,
    )
    gathered = (
        lax.all_gather(local_weights[0], "fsdp", axis=0, tiled=True),
        lax.all_gather(local_weights[1], "fsdp", axis=0, tiled=True),
        lax.all_gather(local_weights[2], "fsdp", axis=0, tiled=True),
        lax.all_gather(local_weights[3], "fsdp", axis=1, tiled=True),
        lax.all_gather(local_weights[4], "fsdp", axis=0, tiled=True),
        lax.all_gather(local_weights[5], "fsdp", axis=0, tiled=True),
        lax.all_gather(local_weights[6], "fsdp", axis=1, tiled=True),
        lax.all_gather(local_weights[7], "fsdp", axis=0, tiled=True),
        lax.all_gather(local_weights[8], "fsdp", axis=0, tiled=True),
        lax.all_gather(local_weights[9], "fsdp", axis=0, tiled=True),
        lax.all_gather(local_weights[10], "fsdp", axis=0, tiled=True),
        lax.all_gather(local_weights[11], "fsdp", axis=1, tiled=True),
        lax.all_gather(local_weights[12], "fsdp", axis=1, tiled=True),
        lax.all_gather(local_weights[13], "fsdp", axis=0, tiled=True),
    )
    (
        gain_one,
        shift_one,
        query_full,
        query_add,
        pair_full,
        value_add,
        output_full,
        output_add,
        gain_two,
        shift_two,
        up_full,
        up_add,
        down_full,
        down_add,
    ) = gathered
    seq_count, group_len, model_width = stream.shape
    token_count = seq_count * group_len
    local_heads = query_full.shape[1] // HD
    offset = lax.axis_index("ctx") * group_len
    token_places = offset + jnp.arange(group_len)
    keep_rows = (
        (token_places[None, :] < lengths[:, None]).astype(jnp.float32).reshape(token_count, 1)
    )
    query_places = offset + jnp.arange(group_len * local_heads) // local_heads
    token_rows = stream.reshape(token_count, model_width).astype(jnp.float32)
    normed_one, unit_one, scaled_one = norm_forward(
        token_rows, gain_one.astype(jnp.float32), shift_one.astype(jnp.float32)
    )
    input_one = normed_one.astype(jnp.bfloat16)
    queries = (
        jnp.dot(input_one, query_full, preferred_element_type=jnp.float32)
        + query_add.reshape(-1).astype(jnp.float32)
    ).astype(jnp.bfloat16)
    pair_add = jnp.concatenate([jnp.zeros_like(value_add), value_add]).astype(jnp.float32)
    key_values = (
        jnp.dot(input_one, pair_full, preferred_element_type=jnp.float32) + pair_add
    ).astype(jnp.bfloat16)
    all_pairs = lax.all_gather(
        key_values.reshape(seq_count, group_len, 2 * HD), "ctx", axis=1, tiled=True
    )
    query_seqs = queries.reshape(seq_count, group_len * local_heads, HD)
    mixture, log_total = lax.map(
        lambda packed: attend(packed[0], packed[1], packed[2], query_places),
        (query_seqs, all_pairs, lengths),
    )
    mixture = mixture.reshape(token_count, local_heads * HD)
    branch = lax.psum(
        jnp.dot(mixture, output_full, preferred_element_type=jnp.float32), "tp"
    ) + output_add.astype(jnp.float32)
    middle = token_rows + branch
    normed_two, unit_two, scaled_two = norm_forward(
        middle, gain_two.astype(jnp.float32), shift_two.astype(jnp.float32)
    )
    input_two = normed_two.astype(jnp.bfloat16)
    hidden_pre = jnp.dot(input_two, up_full, preferred_element_type=jnp.float32) + up_add.reshape(
        -1
    ).astype(jnp.float32)
    hidden = jax.nn.gelu(hidden_pre, approximate=True).astype(jnp.bfloat16)
    feed_branch = lax.psum(
        jnp.dot(hidden, down_full, preferred_element_type=jnp.float32), "tp"
    ) + down_add.astype(jnp.float32)
    result = middle + feed_branch
    totals = lax.psum(
        (
            jnp.sum(keep_rows * result * result),
            jnp.sum(keep_rows * branch * branch),
            jnp.sum(keep_rows * feed_branch * feed_branch),
            jnp.sum(keep_rows),
        ),
        ("fsdp", "ctx"),
    )
    divisor = totals[3] * model_width
    root_means = jnp.sqrt(jnp.stack([totals[0], totals[1], totals[2]]) / divisor)
    grad_total = cotangent.reshape(token_count, model_width).astype(jnp.float32) * keep_rows
    grad_feed = grad_total.astype(jnp.bfloat16)
    down_grad = jnp.einsum("tf,td->fd", hidden, grad_feed, preferred_element_type=jnp.float32)
    down_bias_grad = jnp.sum(grad_feed.astype(jnp.float32), 0)
    grad_hidden = jnp.einsum("td,fd->tf", grad_feed, down_full, preferred_element_type=jnp.float32)
    unused_value, gelu_pull = jax.vjp(
        lambda inner: jax.nn.gelu(inner, approximate=True), hidden_pre
    )
    grad_pre = gelu_pull(grad_hidden)[0].astype(jnp.bfloat16)
    up_grad = jnp.einsum("td,tf->df", input_two, grad_pre, preferred_element_type=jnp.float32)
    up_bias_grad = jnp.sum(grad_pre.astype(jnp.float32), 0).reshape(up_add.shape)
    grad_normed_two = lax.psum(
        jnp.einsum("tf,df->td", grad_pre, up_full, preferred_element_type=jnp.float32), "tp"
    )
    gain_two_grad = jnp.sum(grad_normed_two * unit_two, 0)
    shift_two_grad = jnp.sum(grad_normed_two, 0)
    grad_middle = grad_total + norm_backward(
        grad_normed_two, unit_two, scaled_two, gain_two.astype(jnp.float32)
    )
    grad_branch = grad_middle.astype(jnp.bfloat16)
    output_grad = jnp.einsum("tq,td->qd", mixture, grad_branch, preferred_element_type=jnp.float32)
    output_bias_grad = jnp.sum(grad_branch.astype(jnp.float32), 0)
    grad_mixture = jnp.einsum(
        "td,qd->tq", grad_branch, output_full, preferred_element_type=jnp.float32
    )
    grad_mixture = grad_mixture.astype(jnp.bfloat16).reshape(seq_count, group_len * local_heads, HD)
    grad_query, grad_pairs = lax.map(
        lambda packed: attend_back(
            packed[0], packed[1], packed[2], query_places, packed[3], packed[4]
        ),
        (query_seqs, all_pairs, lengths, log_total, grad_mixture),
    )
    pair_share = lax.psum_scatter(grad_pairs, "ctx", scatter_dimension=1, tiled=True)
    pair_total = lax.psum(pair_share, "tp")
    grad_key_values = pair_total.reshape(token_count, 2 * HD).astype(jnp.bfloat16)
    grad_queries = grad_query.reshape(token_count, local_heads * HD).astype(jnp.bfloat16)
    query_grad = jnp.einsum(
        "td,tq->dq", input_one, grad_queries, preferred_element_type=jnp.float32
    )
    query_bias_grad = jnp.sum(grad_queries.astype(jnp.float32), 0).reshape(query_add.shape)
    pair_grad = jnp.einsum(
        "td,tk->dk", input_one, grad_key_values, preferred_element_type=jnp.float32
    )
    value_bias_grad = jnp.sum(grad_key_values[:, HD:].astype(jnp.float32), 0)
    grad_normed_one = lax.psum(
        jnp.einsum("tq,dq->td", grad_queries, query_full, preferred_element_type=jnp.float32), "tp"
    )
    grad_normed_one = grad_normed_one + jnp.einsum(
        "tk,dk->td", grad_key_values, pair_full, preferred_element_type=jnp.float32
    )
    gain_one_grad = jnp.sum(grad_normed_one * unit_one, 0)
    shift_one_grad = jnp.sum(grad_normed_one, 0)
    stream_grad = grad_middle + norm_backward(
        grad_normed_one, unit_one, scaled_one, gain_one.astype(jnp.float32)
    )
    weight_grads = (
        gain_one_grad,
        shift_one_grad,
        query_grad,
        query_bias_grad,
        pair_grad,
        value_bias_grad,
        output_grad,
        output_bias_grad,
        gain_two_grad,
        shift_two_grad,
        up_grad,
        up_bias_grad,
        down_grad,
        down_bias_grad,
    )
    shares = (
        lax.psum_scatter(weight_grads[0], ("fsdp", "ctx"), scatter_dimension=0, tiled=True),
        lax.psum_scatter(weight_grads[1], ("fsdp", "ctx"), scatter_dimension=0, tiled=True),
        lax.psum_scatter(weight_grads[2], ("fsdp", "ctx"), scatter_dimension=0, tiled=True),
        lax.psum_scatter(weight_grads[3], ("fsdp", "ctx"), scatter_dimension=1, tiled=True),
        lax.psum_scatter(weight_grads[4], ("fsdp", "ctx"), scatter_dimension=0, tiled=True),
        lax.psum_scatter(weight_grads[5], ("fsdp", "ctx"), scatter_dimension=0, tiled=True),
        lax.psum_scatter(weight_grads[6], ("fsdp", "ctx"), scatter_dimension=1, tiled=True),
        lax.psum_scatter(weight_grads[7], ("fsdp", "ctx"), scatter_dimension=0, tiled=True),
        lax.psum_scatter(weight_grads[8], ("fsdp", "ctx"), scatter_dimension=0, tiled=True),
        lax.psum_scatter(weight_grads[9], ("fsdp", "ctx"), scatter_dimension=0, tiled=True),
        lax.psum_scatter(weight_grads[10], ("fsdp", "ctx"), scatter_dimension=0, tiled=True),
        lax.psum_scatter(weight_grads[11], ("fsdp", "ctx"), scatter_dimension=1, tiled=True),
        lax.psum_scatter(weight_grads[12], ("fsdp", "ctx"), scatter_dimension=1, tiled=True),
        lax.psum_scatter(weight_grads[13], ("fsdp", "ctx"), scatter_dimension=0, tiled=True),
    )
    owned = (
        lax.all_gather(shares[0], "ctx", axis=0, tiled=True),
        lax.all_gather(shares[1], "ctx", axis=0, tiled=True),
        lax.all_gather(shares[2], "ctx", axis=0, tiled=True),
        lax.all_gather(shares[3], "ctx", axis=1, tiled=True),
        lax.all_gather(shares[4], "ctx", axis=0, tiled=True),
        lax.all_gather(shares[5], "ctx", axis=0, tiled=True),
        lax.all_gather(shares[6], "ctx", axis=1, tiled=True),
        lax.all_gather(shares[7], "ctx", axis=0, tiled=True),
        lax.all_gather(shares[8], "ctx", axis=0, tiled=True),
        lax.all_gather(shares[9], "ctx", axis=0, tiled=True),
        lax.all_gather(shares[10], "ctx", axis=0, tiled=True),
        lax.all_gather(shares[11], "ctx", axis=1, tiled=True),
        lax.all_gather(shares[12], "ctx", axis=1, tiled=True),
        lax.all_gather(shares[13], "ctx", axis=0, tiled=True),
    )
    return (
        (result * keep_rows).astype(jnp.bfloat16).reshape(stream.shape),
        stream_grad.astype(jnp.bfloat16).reshape(stream.shape),
        owned[0],
        owned[1],
        owned[2],
        owned[3],
        owned[4],
        owned[5],
        owned[6],
        owned[7],
        owned[8],
        owned[9],
        owned[10],
        owned[11],
        owned[12],
        owned[13],
        root_means,
    )


def solution(mesh):
    in_specs = (
        P("fsdp", "ctx", None),
        P("fsdp", "ctx", None),
        P("fsdp"),
        P("fsdp"),
        P("fsdp"),
        P("fsdp", "tp"),
        P("tp", "fsdp"),
        P("fsdp", None),
        P("fsdp"),
        P("tp", "fsdp"),
        P("fsdp"),
        P("fsdp"),
        P("fsdp"),
        P("fsdp", "tp"),
        P("tp", "fsdp"),
        P("tp", "fsdp"),
        P("fsdp"),
    )
    out_specs = (
        P("fsdp", "ctx", None),
        P("fsdp", "ctx", None),
        P("fsdp"),
        P("fsdp"),
        P("fsdp", "tp"),
        P("tp", "fsdp"),
        P("fsdp", None),
        P("fsdp"),
        P("tp", "fsdp"),
        P("fsdp"),
        P("fsdp"),
        P("fsdp"),
        P("fsdp", "tp"),
        P("tp", "fsdp"),
        P("tp", "fsdp"),
        P("fsdp"),
        P(),
    )
    return jax.shard_map(body, mesh=mesh, in_specs=in_specs, out_specs=out_specs, check_vma=False)
```

profile of v0, /device:TPU:0, one launch (start us, length us, event | category | flops | bytes accessed | tf_op | source)
XLA Modules:
  0.0 1541.7 jit_solution(9681924402258202839)
XLA Ops:
  12.2 6.1 all-gather.1
  18.4 5.4 all-gather.2
  25.3 7.3 all-reduce.1
  33.3 2.2 fusion.12
  35.4 5.1 all-gather.3
  40.6 2.6 fusion.45
  43.2 9.2 all-gather
  53.3 4.3 fusion.44
  59.0 2.5 fusion.77
  66.7 10.8 all-gather.30.cloned.1.call-done
  77.5 4.9 fusion.80
  83.6 5.2 all-gather.4
  88.8 5.5 all-gather.5
  94.4 5.2 all-gather.6
  99.6 5.2 all-gather.7
  104.9 132.7 %all-reduce.17.cloned.1.call-done = f32[512,2048]{1,0:T(8,128)} async-done(((f32[512,2048]{1,0:T(8,128)}), f32[512,2048]{1,0:T(8,128)}) %all-reduce.17.cloned.1.call-update) | async-done | bytes 4194320 | tf_op jit(solution)/shard_map/psum | solution.py:172
  237.5 2.8 fusion.75
  242.9 53.4 %all-gather.32.cloned.1.call-done = bf16[2048,2048]{1,0:T(8,128)(2,1)} async-done(((bf16[512,2048]{1,0:T(8,128)(2,1)}), bf16[2048,2048]{1,0:T(8,128)(2,1)}) %all-gather.32.cloned.1.call-update) | async-done | bytes 8388624 | tf_op jit(solution)/shard_map/all_gather | solution.py:120
  296.4 11.3 fusion.73
  307.6 48.5 %all-gather.34.cloned.1.call-done = bf16[2048,2048]{1,0:T(8,128)(2,1)} async-done(((bf16[2048,512]{1,0:T(8,128)(2,1)}), bf16[2048,2048]{1,0:T(8,128)(2,1)}) %all-gather.34.cloned.1.call-update) | async-done | bytes 8388624 | tf_op jit(solution)/shard_map/all_gather | solution.py:122
  356.2 11.7 fusion.71
  367.9 9.3 convert_reduce_fusion.2
  378.6 6.1 fusion.81
  385.4 5.1 all-gather.8
  390.6 285.9 %all-reduce.21.cloned.1.call-done = (f32[512,2048]{1,0:T(8,128)}, f32[512,2048]{1,0:T(8,128)}) async-done(((f32[512,2048]{1,0:T(8,128)}, f32[512,2048]{1,0:T(8,128)}), (f32[512,2048]{1,0:T(8,128)}, f32[512,2048]{1,0:T(8,128)})) %all-reduce.21.cloned.1.call-update) | async-done | bytes 8388624 | tf_op jit(solution)/shard_map/psum | solution.py:184
  676.4 10.8 fusion.27
  687.2 2.1 convert_reduce_fusion.3
  694.9 5.1 fusion.34
  700.0 5.2 multiply_reduce_fusion
  705.3 2.4 multiply_convert_fusion
  712.5 4.3 convolution_convert_fusion
  718.2 3.4 fusion.69
  721.7 5.4 fusion.58
  727.2 13.6 fusion.72
  741.1 14.7 fusion.61
  757.7 4.9 fusion.82
  762.7 28.6 %all-reduce.22 = bf16[1,512,256]{1,2,0:T(8,128)(2,1)S(1)} all-reduce(f32[1,512,256]{1,2,0:T(8,128)} %reduce-scatter.13.cloned.1.call-done), channel_id=1, replica_groups=mesh['fsdp'=4,'ctx'=2,'tp'=4] {'tp'}, use_global_device_ids=true, to_apply=%region_14.15 | all-reduce | flops 131072 | bytes 786432 | tf_op jit(solution)/shard_map/psum | solution.py:232
  791.3 2.5 fusion.67
  794.5 46.9 %reduce-scatter.19.cloned.1.call-done = f32[512,256]{1,0:T(8,128)} async-done(((f32[512,2048]{1,0:T(8,128)}), f32[512,256]{1,0:T(8,128)}) %reduce-scatter.19.cloned.1.call-update) | async-done | bytes 524304 | tf_op jit(solution)/shard_map/reduce_scatter | solution.py:277
  841.4 119.5 %reduce-scatter.21.cloned.1.call-done = f32[256,2048]{1,0:T(8,128)} async-done(((f32[2048,2048]{1,0:T(8,128)}), f32[256,2048]{1,0:T(8,128)}) %reduce-scatter.21.cloned.1.call-update) | async-done | bytes 2097168 | tf_op jit(solution)/shard_map/reduce_scatter | solution.py:281
  961.0 119.3 %reduce-scatter.23.cloned.1.call-done = f32[2048,256]{1,0:T(8,128)} async-done(((f32[2048,2048]{1,0:T(8,128)}), f32[2048,256]{1,0:T(8,128)}) %reduce-scatter.23.cloned.1.call-update) | async-done | bytes 2097168 | tf_op jit(solution)/shard_map/reduce_scatter | solution.py:283
  1084.0 33.0 %reduce-scatter.27.cloned.1.call-done = f32[16,16]{1,0:T(8,128)} async-done(((f32[128,16]{1,0:T(8,128)}), f32[16,16]{1,0:T(8,128)}) %reduce-scatter.27.cloned.1.call-update) | async-done | bytes 1040
  1117.1 4.6 all_gather.113
  1122.3 31.7 %reduce-scatter.25.cloned.1.call-done = f32[16,4]{1,0:T(8,128)} async-done(((f32[128,4]{1,0:T(8,128)}), f32[16,4]{1,0:T(8,128)}) %reduce-scatter.25.cloned.1.call-update) | async-done | bytes 272
  1154.8 4.3 all-gather.11
  1159.9 151.9 %all-reduce.19.cloned.1.call-done = f32[512,2048]{1,0:T(8,128)} async-done(((f32[512,2048]{1,0:T(8,128)}), f32[512,2048]{1,0:T(8,128)}) %all-reduce.19.cloned.1.call-update) | async-done | bytes 4194320 | tf_op jit(solution)/shard_map/psum | solution.py:243
  1311.8 5.5 fusion.18
  1317.3 25.2 %all-reduce.10 = (f32[2048]{0:T(1024)S(1)}, f32[2048]{0:T(1024)S(1)}, f32[128]{0:T(128)S(1)}, f32[2048]{0:T(1024)S(1)}, f32[2048]{0:T(1024)S(1)}, /*index=5*/f32...) all-reduce(f32[2048]{0:T(1024)S(1)} %get-tuple-element.84, ...), channel_id=4, replica_groups=mesh['fsdp'=4,'ctx'=2,'tp'=4] {'fsdp','ctx'}, use_global_device_ids=true, to_apply=%region_18.19.clone | all-reduce | flops 12420 | bytes 99360
  1342.6 4.2 all-gather.9
  1346.9 4.2 all-gather.10
  1351.2 4.2 all-gather.12
  1355.5 4.2 all-gather.13
  1359.8 4.2 all-gather.14
  1364.1 4.2 all-gather.15
  1369.2 5.5 all-reduce.2
  1374.7 2.5 fusion.56
  1377.2 5.3 fusion.42
  1382.5 7.2 all_gather.106
  1389.8 13.6 all-gather.38.cloned.1.call-done
  1403.3 58.3 %all-gather.40.cloned.1.call-done = f32[512,2048]{1,0:T(8,128)} async-done(((f32[256,2048]{1,0:T(8,128)}), f32[512,2048]{1,0:T(8,128)}) %all-gather.40.cloned.1.call-update) | async-done | bytes 4194320 | tf_op jit(solution)/shard_map/all_gather | solution.py:297
  1461.7 58.2 %all-gather.42.cloned.1.call-done = f32[2048,512]{1,0:T(8,128)} async-done(((f32[2048,256]{1,0:T(8,128)}), f32[2048,512]{1,0:T(8,128)}) %all-gather.42.cloned.1.call-update) | async-done | bytes 4194320 | tf_op jit(solution)/shard_map/all_gather | solution.py:299
  1521.0 2.4 copy.69
  1524.2 2.3 copy.71
  1528.2 2.1 copy.75
  (188 shorter events, 46.6 us)
Async XLA Ops:
  7.2 16.6 %copy-start.29 = (u32[32]{0:T(128)S(1)}, u32[32]{0:T(128)}, u32[]{:S(2)}) copy-start(u32[32]{0:T(128)} %constant.110) | copy-start | bytes 388
  7.2 4.3 copy-start.3
  7.2 5.0 copy-start.18
  7.2 11.1 copy-start.19
  7.2 17.8 %copy-start.26 = (bf16[32]{0:T(256)(128)(2,1)S(1)}, bf16[32]{0:T(256)(128)(2,1)}, u32[]{:S(2)}) copy-start(bf16[32]{0:T(256)(128)(2,1)} %param.25) | copy-start | bytes 196
  7.2 33.3 %all-gather.28.cloned.1.call-start = ((), (), s32[]{:S(2)}) async-start(), calls=%async_computation.9 | async-start | bytes 1310720 | tf_op jit(solution)/shard_map/all_gather | solution.py:114
  8.0 45.3 %all-gather.26.cloned.1.call-start = ((), (), s32[]{:S(2)}) async-start(), calls=%async_computation.8 | async-start | bytes 2621440 | tf_op jit(solution)/shard_map/all_gather | solution.py:112
  8.7 68.8 %all-gather.30.cloned.1.call-start = ((), (), s32[]{:S(2)}) async-start(), calls=%async_computation.10 | async-start | bytes 2621440 | tf_op jit(solution)/shard_map/all_gather | solution.py:116
  9.5 228.1 %all-reduce.17.cloned.1.call-start = ((), (), s32[]{:S(2)}) async-start(), calls=%async_computation.11 | async-start | bytes 8388608 | tf_op jit(solution)/shard_map/psum | solution.py:172
  9.5 25.9 %copy-start.20 = (bf16[4,32]{1,0:T(4,128)(2,1)S(1)}, bf16[4,32]{1,0:T(4,128)(2,1)}, u32[]{:S(2)}) copy-start(bf16[4,32]{1,0:T(4,128)(2,1)} %param.23) | copy-start | bytes 772
  52.4 10.3 copy-start.14
  58.9 2.5 copy-start.11
  61.4 3.2 copy-start
  82.4 1.3 copy-start.21
  82.4 6.4 copy-start.22
  82.4 12.0 copy-start.23
  82.4 17.2 %copy-start.17 = (bf16[16,32]{1,0:T(8,128)(2,1)S(1)}, bf16[16,32]{1,0:T(8,128)(2,1)}, u32[]{:S(2)}) copy-start(bf16[16,32]{1,0:T(8,128)(2,1)} %param.31) | copy-start | bytes 3076
  82.4 214.0 %all-gather.32.cloned.1.call-start = ((), (), s32[]{:S(2)}) async-start(), calls=%async_computation.12 | async-start | bytes 10485760 | tf_op jit(solution)/shard_map/all_gather | solution.py:120
  83.0 273.2 %all-gather.34.cloned.1.call-start = ((), (), s32[]{:S(2)}) async-start(), calls=%async_computation.13 | async-start | bytes 10485760 | tf_op jit(solution)/shard_map/all_gather | solution.py:122
  83.6 592.9 %all-reduce.21.cloned.1.call-start = ((), (), s32[]{:S(2)}) async-start(), calls=%async_computation.27 | async-start | bytes 16777216 | tf_op jit(solution)/shard_map/psum | solution.py:184
  240.4 2.0 copy-start.1
  356.2 11.7 copy-start.7
  356.2 11.7 copy-start.25
  356.2 22.4 %slice-start.2 = ((s8[8388608]{0:T(1024)(128)(4,1)}), s8[4194304]{0:T(1024)(128)(4,1)S(1)}, s32[]{:S(2)}) async-start(s8[8388608]{0:T(1024)(128)(4,1)} %bitcast.195), calls=%async_computation.30 | async-start | bytes 8388608
  367.9 10.7 slice-start.3
  377.2 1.3 copy-start.30
  384.7 0.7 copy-start.24
  384.7 378.0 %reduce-scatter.13.cloned.1.call-start = ((), (), s32[]{:S(2)}) async-start(), calls=%async_computation.15 | async-start | bytes 1572864 | tf_op jit(solution)/shard_map/reduce_scatter | solution.py:231
  676.4 10.8 copy-start.2
  676.4 10.8 copy-start.6
  676.4 10.8 copy-start.8
  687.2 4.2 copy-start.13
  689.4 2.0 copy-start.4
  694.9 5.1 copy-start.15
  694.9 10.3 slice-start
  700.0 5.3 slice-start.1
  705.2 4.4 copy-start.12
  707.7 1.9 copy-start.5
  709.6 2.9 copy-start.16
  712.2 81.7 %reduce-scatter.15.cloned.1.call-start = ((), (), s32[]{:S(2)}) async-start(), calls=%async_computation.16 | async-start | bytes 4718592 | tf_op jit(solution)/shard_map/reduce_scatter | solution.py:273
  721.7 119.7 %reduce-scatter.19.cloned.1.call-start = ((), (), s32[]{:S(2)}) async-start(), calls=%async_computation.19 | async-start | bytes 4718592 | tf_op jit(solution)/shard_map/reduce_scatter | solution.py:277
  727.2 233.7 %reduce-scatter.21.cloned.1.call-start = ((), (), s32[]{:S(2)}) async-start(), calls=%async_computation.21 | async-start | bytes 18874368 | tf_op jit(solution)/shard_map/reduce_scatter | solution.py:281
  740.8 339.4 %reduce-scatter.23.cloned.1.call-start = ((), (), s32[]{:S(2)}) async-start(), calls=%async_computation.23 | async-start | bytes 18874368 | tf_op jit(solution)/shard_map/reduce_scatter | solution.py:283
  755.9 361.2 %reduce-scatter.27.cloned.1.call-start = ((), (), s32[]{:S(2)}) async-start(), calls=%async_computation.26 | async-start | bytes 73728
  756.7 397.3 %reduce-scatter.25.cloned.1.call-start = ((), (), s32[]{:S(2)}) async-start(), calls=%async_computation.25 | async-start | bytes 73728
  757.6 554.2 %all-reduce.19.cloned.1.call-start = ((), (), s32[]{:S(2)}) async-start(), calls=%async_computation.14 | async-start | bytes 8388608 | tf_op jit(solution)/shard_map/psum | solution.py:243
  762.6 619.9 %reduce-scatter.17.cloned.1.call-start = ((), (), s32[]{:S(2)}) async-start(), calls=%async_computation.18 | async-start | bytes 2359296 | tf_op jit(solution)/shard_map/reduce_scatter | solution.py:275
  793.8 286.5 %copy-start.28 = (u32[32]{0:T(128)S(1)}, u32[32]{0:T(128)}, u32[]{:S(2)}) copy-start(u32[32]{0:T(128)} %constant.115) | copy-start | bytes 388
  793.8 287.1 %copy-start.27 = (u32[32]{0:T(128)S(1)}, u32[32]{0:T(128)}, u32[]{:S(2)}) copy-start(u32[32]{0:T(128)} %constant.122) | copy-start | bytes 388
  793.8 595.9 %all-gather.36.cloned.1.call-start = ((), (), s32[]{:S(2)}) async-start(), calls=%async_computation.17 | async-start | bytes 1572864 | tf_op jit(solution)/shard_map/all_gather | solution.py:289
  794.4 608.9 %all-gather.38.cloned.1.call-start = ((), (), s32[]{:S(2)}) async-start(), calls=%async_computation.20 | async-start | bytes 1572864 | tf_op jit(solution)/shard_map/all_gather | solution.py:293
  841.4 620.3 %all-gather.40.cloned.1.call-start = ((), (), s32[]{:S(2)}) async-start(), calls=%async_computation.22 | async-start | bytes 6291456 | tf_op jit(solution)/shard_map/all_gather | solution.py:297
  960.9 558.9 %all-gather.42.cloned.1.call-start = ((), (), s32[]{:S(2)}) async-start(), calls=%async_computation.24 | async-start | bytes 6291456 | tf_op jit(solution)/shard_map/all_gather | solution.py:299
  1519.8 8.3 copy-start.9
  1528.2 3.7 copy-start.10
Sparse Core Ops, SparseCore 0:
  9.6 19.4 all-gather.27
  30.7 22.5 all-gather.25
  54.9 22.5 all-gather.29
  82.5 154.9 all-reduce.16
  239.0 57.2 all-gather.31
  297.9 58.2 all-gather.33
  384.9 291.5 all-reduce.20
  712.3 19.3 reduce-scatter.12
  735.0 51.3 reduce-scatter.14
  790.0 51.3 reduce-scatter.18
  844.9 115.9 reduce-scatter.20
  964.3 115.9 reduce-scatter.22
  1083.8 33.1 reduce-scatter.26
  1120.8 33.1 reduce-scatter.24
  1156.8 154.9 all-reduce.18
  1315.9 40.4 reduce-scatter.16
  1357.8 21.6 all-gather.35
  1380.9 22.3 all-gather.37
  1404.9 56.7 all-gather.39
  1463.1 56.7 all-gather.41
where the time goes:
time: 1550 us; the launch traced here: 1540 us
  waiting for transfers between devices  1170 us (75%)
  blocking collectives  160 us (10%)
  matrix products  123 us (8%)
  local copies, waits for them, and re-layouts  35.5 us (2%)
  other arithmetic  34.4 us (2%)
  between operations  19.3 us (1%)
    psum x1, waiting for transfers between devices, body(): lax.psum(jnp.dot(hidden, down_full, preferred_element_type=jnp.float32),...  286 us
    psum x1, waiting for transfers between devices, body(): lax.psum(jnp.einsum('tq,dq->td', grad_queries, query_full, preferred_elem...  152 us
    psum x1, waiting for transfers between devices, body(): lax.psum(jnp.dot(mixture, output_full, preferred_element_type=jnp.float32...  133 us
    reduce_scatter x1, waiting for transfers between devices, body(): lax.psum_scatter(weight_grads[10], ('fsdp', 'ctx'), scatter_dimension=0,...  119 us
    reduce_scatter x1, waiting for transfers between devices, body(): lax.psum_scatter(weight_grads[12], ('fsdp', 'ctx'), scatter_dimension=1,...  119 us
    unnamed x22, waiting for transfers between devices  68.6 us
    all_gather x1, waiting for transfers between devices, body(): lax.all_gather(shares[10], 'ctx', axis=0, tiled=True)  58.3 us
    all_gather x1, waiting for transfers between devices, body(): lax.all_gather(shares[12], 'ctx', axis=1, tiled=True)  58.2 us
  transfers between devices with their start and end apart: 20, of which 15 were waited for; matrix products, arithmetic and copies ran while one was open for 7% of the time, Pallas kernels for 0%

commit v1 on v0

v1 whole, which is shorter than its diff:
```python
import math

import jax
import jax.numpy as jnp
from jax import lax
from jax.sharding import PartitionSpec as P

HD = 128


EPSILON = 1e-05
NEGATIVE = -1e30


def norm_forward(inputs, norm_gain, norm_shift):
    center = inputs - jnp.mean(inputs, -1, keepdims=True)
    spread = jnp.mean(center * center, -1, keepdims=True)
    scaled = lax.rsqrt(spread + EPSILON)
    unit_rows = center * scaled
    return (unit_rows * norm_gain + norm_shift, unit_rows, scaled)


def norm_backward(upstream, unit_rows, scaled, norm_gain):
    gained = upstream * norm_gain
    return scaled * (
        gained
        - jnp.mean(gained, -1, keepdims=True)
        - unit_rows * jnp.mean(gained * unit_rows, -1, keepdims=True)
    )


def score_block(query_block, key_rows, length, query_places):
    raw_scores = jnp.einsum("qd,kd->qk", query_block, key_rows, preferred_element_type=jnp.float32)
    key_places = jnp.arange(key_rows.shape[0])
    allowed = (key_places[None, :] <= query_places[:, None]) & (key_places[None, :] < length)
    return jnp.where(allowed, raw_scores * (1.0 / math.sqrt(HD)), NEGATIVE)


def attend(query_block, pair_block, length, query_places):
    scores = score_block(query_block, pair_block[:, :HD], length, query_places)
    peak = jnp.max(scores, -1, keepdims=True)
    exponent = jnp.exp(scores - peak)
    row_total = jnp.sum(exponent, -1, keepdims=True)
    soft_weights = (exponent / row_total).astype(jnp.bfloat16)
    mixture = jnp.dot(soft_weights, pair_block[:, HD:], preferred_element_type=jnp.float32)
    return (mixture.astype(jnp.bfloat16), (peak + jnp.log(row_total))[:, 0])


def attend_back(query_block, pair_block, length, query_places, log_total, grad_mixture):
    key_rows = pair_block[:, :HD]
    value_rows = pair_block[:, HD:]
    scores = score_block(query_block, key_rows, length, query_places)
    soft_weights = jnp.exp(scores - log_total[:, None])
    grad_weights = jnp.einsum(
        "qd,kd->qk", grad_mixture, value_rows, preferred_element_type=jnp.float32
    )
    row_dot = jnp.sum(soft_weights * grad_weights, -1, keepdims=True)
    grad_scores = (soft_weights * (grad_weights - row_dot) * (1.0 / math.sqrt(HD))).astype(
        jnp.bfloat16
    )
    grad_query = jnp.dot(grad_scores, key_rows, preferred_element_type=jnp.float32)
    grad_keys = jnp.einsum(
        "qk,qd->kd", grad_scores, query_block, preferred_element_type=jnp.float32
    )
    grad_values = jnp.einsum(
        "qk,qd->kd",
        soft_weights.astype(jnp.bfloat16),
        grad_mixture,
        preferred_element_type=jnp.float32,
    )
    return (grad_query, jnp.concatenate([grad_keys, grad_values], -1))


def swap(block, axis, bit):
    count = lax.axis_size(axis)
    return lax.ppermute(block, axis, [(place, place ^ bit) for place in range(count)])


def bits_of(axis):
    count, bit, found = lax.axis_size(axis), 1, []
    while bit < count:
        found.append(bit)
        bit *= 2
    return found


def pick(array, index, size, axis):
    return lax.dynamic_slice_in_dim(array, index * size, size, axis)


def over_ctx(part, axis):
    held = [(0, part)]
    for bit in bits_of("ctx"):
        held = held + [(mask ^ bit, swap(block, "ctx", bit)) for mask, block in held]
    place = lax.axis_index("ctx")
    size = part.shape[axis]
    shape = list(part.shape)
    shape[axis] = size * len(held)
    whole = jnp.zeros(shape, part.dtype)
    for mask, block in held:
        whole = lax.dynamic_update_slice_in_dim(whole, block, (place ^ mask) * size, axis)
    return whole


def gather_blocks(shard):
    count, split = lax.axis_size("fsdp"), lax.axis_size("ctx")
    blocks = {0: shard}
    for bit in bits_of("fsdp"):
        if bit == 1:
            blocks[1] = swap(shard, "fsdp", 1)
        else:
            size = shard.shape[0] // split
            part = pick(shard, lax.axis_index("ctx"), size, 0)
            for mask in [m for m in list(blocks) if m < bit and m % 2 == 0]:
                source = part if mask == 0 else pick(blocks[mask], lax.axis_index("ctx"), size, 0)
                blocks[mask ^ bit] = over_ctx(swap(source, "fsdp", bit), 0)
                blocks[mask ^ bit ^ 1] = swap(blocks[mask ^ bit], "fsdp", 1)
    return [blocks[r] for r in range(count)]


def join_blocks(blocks, axis):
    place = lax.axis_index("fsdp")
    size = blocks[0].shape[axis]
    shape = list(blocks[0].shape)
    shape[axis] = size * len(blocks)
    whole = jnp.zeros(shape, blocks[0].dtype)
    for r, block in enumerate(blocks):
        whole = lax.dynamic_update_slice_in_dim(whole, block, (place ^ r) * size, axis)
    return whole


def reduce_blocks(parts):
    held = list(parts)
    for bit in bits_of("fsdp"):
        kept = {}
        for r in range(len(held)):
            if held[r] is None or not r & bit:
                continue
            came = swap(held[r].astype(jnp.bfloat16), "fsdp", bit)
            kept[r ^ bit] = came
            held[r] = None
        for r, came in kept.items():
            held[r] = held[r] + came.astype(jnp.float32)
    total = held[0]
    for bit in bits_of("ctx"):
        sent = total.astype(jnp.bfloat16)
        total = sent.astype(jnp.float32) + swap(sent, "ctx", bit).astype(jnp.float32)
    return total


def line_reduce(own):
    count, place = lax.axis_size("tp"), lax.axis_index("tp")
    right = left = None
    for step in range(1, count):
        index = jnp.minimum(count - step + place, count - 1)
        value = lax.dynamic_index_in_dim(own, index, 0, False)
        if right is not None:
            value = (value.astype(jnp.float32) + right.astype(jnp.float32)).astype(own.dtype)
        right = lax.ppermute(value, "tp", [(i, i + 1) for i in range(step)])
        index = jnp.maximum(place - (count - step), 0)
        value = lax.dynamic_index_in_dim(own, index, 0, False)
        if left is not None:
            value = (value.astype(jnp.float32) + left.astype(jnp.float32)).astype(own.dtype)
        left = lax.ppermute(value, "tp", [(count - 1 - i, count - 2 - i) for i in range(step)])
    total = lax.dynamic_index_in_dim(own, place, 0, False).astype(jnp.float32)
    return total + right.astype(jnp.float32) + left.astype(jnp.float32)


def line_gather(own):
    count, place = lax.axis_size("tp"), lax.axis_index("tp")
    rights, lefts = [], []
    right = left = own
    for step in range(1, count):
        right = lax.ppermute(right, "tp", [(i, i + 1) for i in range(step - 1, count - 1)])
        left = lax.ppermute(
            left, "tp", [(count - 1 - i, count - 2 - i) for i in range(step - 1, count - 1)]
        )
        rights.append(right)
        lefts.append(left)
    stacked = jnp.concatenate(rights[::-1] + [own] + lefts, 0)
    size = own.shape[0]
    return lax.dynamic_slice_in_dim(stacked, (count - 1 - place) * size, count * size, 0)


def sum_over(values, axes):
    for axis in axes:
        for bit in bits_of(axis):
            values = values + swap(values, axis, bit)
    return values


def body(
    stream,
    cotangent,
    lengths,
    first_gain,
    first_shift,
    query_weight,
    query_bias,
    pair_weight,
    value_bias,
    output_weight,
    output_bias,
    second_gain,
    second_shift,
    up_weight,
    up_bias,
    down_weight,
    down_bias,
):
    low, wide = jnp.bfloat16, jnp.float32
    fsdp, tp = lax.axis_size("fsdp"), lax.axis_size("tp")
    me, place, zone = lax.axis_index("fsdp"), lax.axis_index("ctx"), lax.axis_index("tp")
    seq_count, group_len, model_width = stream.shape
    token_count = seq_count * group_len
    local_heads = query_weight.shape[1] // HD
    share = token_count // tp

    smalls = (first_gain, first_shift, output_bias, second_gain, second_shift, down_bias)
    piece = first_gain.shape[0]
    flat = [s for s in smalls] + [query_bias.reshape(-1), value_bias, up_bias.reshape(-1)]
    packed = jnp.concatenate(flat)
    small_blocks = [packed]
    for bit in bits_of("fsdp"):
        small_blocks = small_blocks + [swap(block, "fsdp", bit) for block in small_blocks]
    small_all = join_blocks([block[None] for block in small_blocks], 0)
    offsets, start = [], 0
    for s in flat:
        offsets.append((start, s.size))
        start += s.size

    def small(index):
        start, size = offsets[index]
        return small_all[:, start : start + size]

    gain_one, shift_one, output_add, gain_two, shift_two, down_add = [
        small(k).reshape(-1).astype(wide) for k in range(6)
    ]
    query_add = (
        small(6).reshape((fsdp,) + query_bias.shape).transpose(1, 0, 2).reshape(-1).astype(wide)
    )
    value_add = small(7).reshape(-1)
    up_add = small(8).reshape((fsdp,) + up_bias.shape).transpose(1, 0, 2).reshape(-1).astype(wide)

    query_full = join_blocks(gather_blocks(query_weight), 0)
    pair_full = join_blocks(gather_blocks(pair_weight), 0)
    output_full = join_blocks(gather_blocks(output_weight), 1)
    up_full = join_blocks(gather_blocks(up_weight), 0)
    down_full = join_blocks(gather_blocks(down_weight), 1)

    offset = place * group_len
    token_places = offset + jnp.arange(group_len)
    keep_rows = (token_places[None, :] < lengths[:, None]).astype(wide).reshape(token_count, 1)
    keep_share = pick(keep_rows, zone, share, 0)
    query_places = offset + jnp.arange(group_len * local_heads) // local_heads
    flat_stream = stream.reshape(token_count, model_width)
    token_rows = flat_stream.astype(wide)
    normed_one, unit_one, scaled_one = norm_forward(token_rows, gain_one, shift_one)
    input_one = normed_one.astype(low)
    queries = (jnp.dot(input_one, query_full, preferred_element_type=wide) + query_add).astype(low)
    pair_add = jnp.concatenate([jnp.zeros_like(value_add), value_add]).astype(wide)
    key_values = (jnp.dot(input_one, pair_full, preferred_element_type=wide) + pair_add).astype(low)
    all_pairs = over_ctx(key_values.reshape(seq_count, group_len, 2 * HD), 1)
    query_seqs = queries.reshape(seq_count, group_len * local_heads, HD)
    mixture, log_total = lax.map(
        lambda packed: attend(packed[0], packed[1], packed[2], query_places),
        (query_seqs, all_pairs, lengths),
    )
    mixture = mixture.reshape(token_count, local_heads * HD)
    stream_share = pick(flat_stream, zone, share, 0).astype(wide)
    branch_part = jnp.dot(mixture, output_full, preferred_element_type=wide).astype(low)
    branch = line_reduce(branch_part.reshape(tp, share, model_width)) + output_add
    middle = stream_share + branch
    normed_two, unit_two, scaled_two = norm_forward(middle, gain_two, shift_two)
    input_two = line_gather(normed_two.astype(low))

    grad_total = cotangent.reshape(token_count, model_width).astype(wide) * keep_rows
    grad_feed = grad_total.astype(low)
    grad_total_share = pick(grad_total, zone, share, 0)
    hidden_pre = jnp.dot(input_two, up_full, preferred_element_type=wide) + up_add
    hidden = jax.nn.gelu(hidden_pre, approximate=True).astype(low)
    feed_part = jnp.dot(hidden, down_full, preferred_element_type=wide).astype(low)
    grad_hidden = jnp.einsum("td,fd->tf", grad_feed, down_full, preferred_element_type=wide)
    unused_value, gelu_pull = jax.vjp(
        lambda inner: jax.nn.gelu(inner, approximate=True), hidden_pre
    )
    grad_pre = gelu_pull(grad_hidden)[0].astype(low)
    grad_two_part = jnp.einsum("tf,df->td", grad_pre, up_full, preferred_element_type=wide).astype(
        low
    )
    columns = model_width // fsdp

    def turned(rows, r):
        return pick(rows, me ^ r, columns, 1)

    down_grad = reduce_blocks(
        [
            jnp.einsum("tf,td->fd", hidden, turned(grad_feed, r), preferred_element_type=wide)
            for r in range(fsdp)
        ]
    )
    up_grad = reduce_blocks(
        [
            jnp.einsum("td,tf->df", turned(input_two, r), grad_pre, preferred_element_type=wide)
            for r in range(fsdp)
        ]
    )
    grad_normed_two = line_reduce(grad_two_part.reshape(tp, share, model_width))
    grad_middle = grad_total_share + norm_backward(grad_normed_two, unit_two, scaled_two, gain_two)
    grad_branch_share = grad_middle.astype(low)
    grad_branch = line_gather(grad_branch_share)
    output_grad = reduce_blocks(
        [
            jnp.einsum("tq,td->qd", mixture, turned(grad_branch, r), preferred_element_type=wide)
            for r in range(fsdp)
        ]
    )
    grad_mixture = jnp.einsum("td,qd->tq", grad_branch, output_full, preferred_element_type=wide)
    grad_mixture = grad_mixture.astype(low).reshape(seq_count, group_len * local_heads, HD)
    grad_query, grad_pairs = lax.map(
        lambda packed: attend_back(
            packed[0], packed[1], packed[2], query_places, packed[3], packed[4]
        ),
        (query_seqs, all_pairs, lengths, log_total, grad_mixture),
    )
    pair_part = pick(grad_pairs, place, group_len, 1)
    ctx = lax.axis_size("ctx")
    for other in range(1, ctx):
        sent = pick(grad_pairs, lax.rem(place + other, ctx), group_len, 1).astype(low)
        pair_part = pair_part + lax.ppermute(
            sent, "ctx", [(i, (i + other) % ctx) for i in range(ctx)]
        ).astype(wide)
    pair_share = line_reduce(pair_part.astype(low).reshape(tp, share, 2 * HD)).astype(low)
    grad_key_values = line_gather(pair_share)
    grad_queries = grad_query.reshape(token_count, local_heads * HD).astype(low)
    query_grad = reduce_blocks(
        [
            jnp.einsum("td,tq->dq", turned(input_one, r), grad_queries, preferred_element_type=wide)
            for r in range(fsdp)
        ]
    )
    pair_grad = reduce_blocks(
        [
            jnp.einsum(
                "td,tk->dk", turned(input_one, r), grad_key_values, preferred_element_type=wide
            )
            for r in range(fsdp)
        ]
    )
    grad_one_part = jnp.einsum(
        "tq,dq->td", grad_queries, query_full, preferred_element_type=wide
    ).astype(low)
    grad_normed_one = line_reduce(grad_one_part.reshape(tp, share, model_width)) + jnp.einsum(
        "tk,dk->td", pair_share, pair_full, preferred_element_type=wide
    )
    unit_share = pick(unit_one, zone, share, 0)
    scaled_share = pick(scaled_one, zone, share, 0)
    stream_grad = grad_middle + norm_backward(grad_normed_one, unit_share, scaled_share, gain_one)
    stream_grad = line_gather(stream_grad.astype(low))

    feed_branch = line_reduce(feed_part.reshape(tp, share, model_width)) + down_add
    total = middle + feed_branch
    result = line_gather((total * keep_share).astype(low))

    shared = jnp.concatenate(
        [
            jnp.sum(grad_normed_two * unit_two, 0),
            jnp.sum(grad_normed_two, 0),
            jnp.sum(grad_branch_share.astype(wide), 0),
            jnp.sum(pick(grad_feed, zone, share, 0).astype(wide), 0),
            jnp.stack(
                [
                    jnp.sum(keep_share * total * total),
                    jnp.sum(keep_share * branch * branch),
                    jnp.sum(keep_share * feed_branch * feed_branch),
                    jnp.sum(keep_share),
                ]
            ),
        ]
    )
    shared = sum_over(shared, ("tp", "fsdp", "ctx"))
    late = jnp.concatenate(
        [
            jnp.sum(grad_normed_one * unit_share, 0),
            jnp.sum(grad_normed_one, 0),
            jnp.sum(pair_share[:, HD:].astype(wide), 0),
        ]
    )
    late = sum_over(late, ("tp", "fsdp", "ctx"))
    own = jnp.concatenate(
        [jnp.sum(grad_pre.astype(wide), 0), jnp.sum(grad_queries.astype(wide), 0)]
    )
    own = sum_over(own, ("fsdp", "ctx"))
    up_bias_all = own[: up_add.shape[0]].reshape(up_bias.shape[0], fsdp, -1)
    query_bias_all = own[up_add.shape[0] :].reshape(query_bias.shape[0], fsdp, -1)
    width = model_width

    def mine(row, size):
        return pick(row, me, size, 0)

    totals = shared[4 * width :]
    root_means = jnp.sqrt(totals[:3] / (totals[3] * width))
    return (
        result.reshape(stream.shape),
        stream_grad.reshape(stream.shape),
        mine(late[:width], piece),
        mine(late[width : 2 * width], piece),
        query_grad,
        lax.dynamic_index_in_dim(query_bias_all, me, 1, False),
        pair_grad,
        mine(late[2 * width :], value_bias.shape[0]),
        output_grad,
        mine(shared[2 * width : 3 * width], piece),
        mine(shared[:width], piece),
        mine(shared[width : 2 * width], piece),
        up_grad,
        lax.dynamic_index_in_dim(up_bias_all, me, 1, False),
        down_grad,
        mine(shared[3 * width : 4 * width], piece),
        root_means,
    )


def solution(mesh):
    in_specs = (
        P("fsdp", "ctx", None),
        P("fsdp", "ctx", None),
        P("fsdp"),
        P("fsdp"),
        P("fsdp"),
        P("fsdp", "tp"),
        P("tp", "fsdp"),
        P("fsdp", None),
        P("fsdp"),
        P("tp", "fsdp"),
        P("fsdp"),
        P("fsdp"),
        P("fsdp"),
        P("fsdp", "tp"),
        P("tp", "fsdp"),
        P("tp", "fsdp"),
        P("fsdp"),
    )
    out_specs = (
        P("fsdp", "ctx", None),
        P("fsdp", "ctx", None),
        P("fsdp"),
        P("fsdp"),
        P("fsdp", "tp"),
        P("tp", "fsdp"),
        P("fsdp", None),
        P("fsdp"),
        P("tp", "fsdp"),
        P("fsdp"),
        P("fsdp"),
        P("fsdp"),
        P("fsdp", "tp"),
        P("tp", "fsdp"),
        P("tp", "fsdp"),
        P("fsdp"),
        P(),
    )
    return jax.shard_map(body, mesh=mesh, in_specs=in_specs, out_specs=out_specs, check_vma=False)
```

time: 1550 us -> 698 us (0.45)
  waiting for transfers between devices: 1170 us -> 261 us
  starting transfers between devices: 1.27 us -> 185 us
  blocking collectives: 160 us -> 0 us
  local copies, waits for them, and re-layouts: 35.5 us -> 86.7 us
  matrix products: 123 us -> 100 us
  other arithmetic: 34.4 us -> 53.8 us
    psum x3 -> x0, waiting for transfers between devices: 570 us -> none  [the longest x1 286 us: body(): lax.psum(jnp.dot(hidden, down_full, preferred_element_type=jnp.float32),...]
    reduce_scatter x6 -> x0, waiting for transfers between devices: 286 us -> none  [the longest x1 119 us: body(): lax.psum_scatter(weight_grads[10], ('fsdp', 'ctx'), scatter_dimension=0,...]
    ppermute x0 -> x118, waiting for transfers between devices: none -> 261 us  [the longest x57 133 us: swap(): lax.ppermute(block, axis, [(place, place ^ bit) for place in range(count)])]
    all_gather x9 -> x0, waiting for transfers between devices: 244 us -> none  [the longest x1 58.3 us: body(): lax.all_gather(shares[10], 'ctx', axis=0, tiled=True)]
    ppermute x0 -> x118, starting transfers between devices: none -> 185 us  [the longest x15 68.3 us: line_reduce(): right = lax.ppermute(value, 'tp', [(i, i + 1) for i in range(step)])]
    all_gather x18 -> x0, blocking collectives: 93.5 us -> none  [the longest x1 9.21 us: body(): lax.all_gather(key_values.reshape(seq_count, group_len, 2 * HD), 'ctx', a...]
    unnamed x22 -> x0, waiting for transfers between devices: 68.6 us -> none
    unnamed x3 -> x0, blocking collectives: 38 us -> none
  transfers between devices with their start and end apart: 20 -> 118, of which waited for: 15 -> 48; matrix products, arithmetic and copies ran while one was open for 7% -> 29% of each run, Pallas kernels for 0% -> 0%
where the time goes in v1:
time: 698 us; the launch traced here: 692 us
  waiting for transfers between devices  261 us (37%)
  starting transfers between devices  185 us (27%)
  matrix products  100 us (14%)
  local copies, waits for them, and re-layouts  86.7 us (12%)
  other arithmetic  53.8 us (8%)
    ppermute x57, waiting for transfers between devices, swap(): lax.ppermute(block, axis, [(place, place ^ bit) for place in range(count)])  133 us
    ppermute x15, waiting for transfers between devices, line_gather(): lax.ppermute(left, 'tp', [(count - 1 - i, count - 2 - i) for i in range(s...  86.5 us
    ppermute x15, starting transfers between devices, line_reduce(): right = lax.ppermute(value, 'tp', [(i, i + 1) for i in range(step)])  68.3 us
    ppermute x57, starting transfers between devices, swap(): lax.ppermute(block, axis, [(place, place ^ bit) for place in range(count)])  51 us
    ppermute x15, starting transfers between devices, line_gather(): lax.ppermute(right, 'tp', [(i, i + 1) for i in range(step - 1, count - 1)])  27.5 us
    ppermute x15, waiting for transfers between devices, line_reduce(): right = lax.ppermute(value, 'tp', [(i, i + 1) for i in range(step)])  26.5 us
    ppermute x15, starting transfers between devices, line_gather(): lax.ppermute(left, 'tp', [(count - 1 - i, count - 2 - i) for i in range(s...  19.7 us
    dynamic_update_slice x23, local copies, waits for them, and re-layouts, join_blocks(): lax.dynamic_update_slice_in_dim(whole, block, (place ^ r) * size, axis)  18.3 us
  transfers between devices with their start and end apart: 118, of which 48 were waited for; matrix products, arithmetic and copies ran while one was open for 29% of the time, Pallas kernels for 0%

profile of v1, /device:TPU:0, one launch (start us, length us, event | category | flops | bytes accessed | tf_op | source)
XLA Modules:
  0.0 691.8 jit_solution(8284118852657768339)
XLA Ops:
  2.3 4.9 concatenate.34
  25.6 4.2 fusion.4
  51.0 3.1 collective-permute-done.14
  77.4 2.8 convolution_convert_fusion.7
  82.6 4.3 collective-permute-start.16
  95.2 3.1 collective-permute-done.16
  100.3 5.3 collective-permute-start.17
  105.7 4.8 convert_multiply_fusion
  122.8 3.4 copy-done.4
  126.4 11.1 %collective-permute-done.33 = bf16[1024,512]{1,0:T(8,128)(2,1)} collective-permute-done((bf16[1024,512]{1,0:T(8,128)(2,1)}, bf16[1024,512]{1,0:T(8,128)(2,1)}, u32[]{:S(2)}, u32[]{:S(2)}) %collective-permute-start.33) | collective-permute-done | bytes 1048608 | tf_op jit(solution)/shard_map/ppermute | solution.py:76
  149.8 12.5 %collective-permute-done.34 = bf16[1024,512]{1,0:T(8,128)(2,1)S(1)} collective-permute-done((bf16[1024,512]{1,0:T(8,128)(2,1)}, bf16[1024,512]{1,0:T(8,128)(2,1)S(1)}, u32[]{:S(2)}, u32[]{:S(2)}) %collective-permute-start.34) | collective-permute-done | bytes 1048608 | tf_op jit(solution)/shard_map/ppermute | solution.py:76
  170.6 6.5 collective-permute-done.22
  178.5 6.5 collective-permute-done.25
  188.1 6.1 fusion.143
  194.3 5.8 collective-permute-done.26
  206.2 8.1 %collective-permute-done.27 = bf16[128,2048]{1,0:T(8,128)(2,1)S(1)} collective-permute-done((bf16[128,2048]{1,0:T(8,128)(2,1)}, bf16[128,2048]{1,0:T(8,128)(2,1)S(1)}, u32[]{:S(2)}, u32[]{:S(2)}) %collective-permute-start.27) | collective-permute-done | bytes 524320 | tf_op jit(solution)/shard_map/ppermute | solution.py:175
  214.3 8.8 %convert_reduce_fusion.1 = (f32[2048]{0:T(1024)S(1)}, bf16[512,2048]{1,0:T(8,128)(2,1)}, bf16[512,2048]{1,0:T(8,128)(2,1)S(1)}) fusion(f32[512,2048]{1,0:T(8,128)S(1)} %copy-done.79, f32[2048]{0:T(1024)S(1)} %reshape.376, bf16[2048,2048]{1,0:T(8,128)(2,1)S(1)} %constant_dynamic-update-slice_fusion.41, ...), kind=kOutput, calls=%fused_computation.33 | convolution fusion | flops 4321179648 | bytes 18890756 | tf_op jit(solution)/shard_map/dot_general | solution.py:280
  223.1 7.4 %convolution_convert_fusion.5 = bf16[512,2048]{1,0:T(8,128)(2,1)S(1)} fusion(bf16[512,2048]{1,0:T(8,128)(2,1)} %get-tuple-element.83, bf16[2048,2048]{1,0:T(8,128)(2,1)S(1)} %constant_dynamic-update-slice_fusion.41), kind=kOutput, calls=%fused_computation.43 | convolution fusion | flops 4296015872 | bytes 12582912 | tf_op jit(solution)/shard_map/tf,df->td/dot_general | solution.py:288
  233.0 4.8 convolution_convert_fusion.6
  246.2 5.2 collective-permute-start.49
  251.4 5.1 collective-permute-done.36
  257.5 5.2 collective-permute-start.37
  270.3 5.1 collective-permute-done.37
  277.7 5.0 collective-permute-start.50
  282.8 4.6 collective-permute-start.38
  290.8 3.7 convolution_convert_fusion
  294.5 3.9 convolution_convert_fusion.2
  298.9 2.9 collective-permute-done.38
  302.6 7.4 %collective-permute-done.41 = bf16[128,2048]{1,0:T(8,128)(2,1)S(1)} collective-permute-done((bf16[128,2048]{1,0:T(8,128)(2,1)S(1)}, bf16[128,2048]{1,0:T(8,128)(2,1)S(1)}, u32[]{:S(2)}, u32[]{:S(2)}) %collective-permute-start.41) | collective-permute-done | bytes 524320 | tf_op jit(solution)/shard_map/ppermute | solution.py:164
  310.0 3.9 fusion.36
  313.9 3.0 convert_reduce_fusion.3
  319.6 6.8 collective-permute-start.105
  328.6 4.9 fusion.73
  339.4 3.9 convolution_convert_fusion.3
  343.3 7.1 %collective-permute-start.42 = (bf16[128,2048]{1,0:T(8,128)(2,1)S(1)}, bf16[128,2048]{1,0:T(8,128)(2,1)S(1)}, u32[]{:S(2)}, u32[]{:S(2)}) collective-permute-start(bf16[128,2048]{1,0:T(8,128)(2,1)S(1)} %copy-done.39), channel_id=1, source_target_pairs={{0,1},{1,2},{2,3},{4,5},{5,6},{6,7},{8,9},{9,10},{10,11},{12,13},{... | collective-permute-start | bytes 1572872 | tf_op jit(solution)/shard_map/ppermute | solution.py:174
  351.1 4.3 add_convert_fusion.1
  360.4 4.6 add_convert_fusion.3
  373.6 8.4 %collective-permute-done.58 = bf16[128,2048]{1,0:T(8,128)(2,1)S(1)} collective-permute-done((bf16[128,2048]{1,0:T(8,128)(2,1)S(1)}, bf16[128,2048]{1,0:T(8,128)(2,1)S(1)}, u32[]{:S(2)}, u32[]{:S(2)}) %collective-permute-start.58) | collective-permute-done | bytes 524320 | tf_op jit(solution)/shard_map/ppermute | solution.py:175
  386.4 12.4 %collective-permute-done.46 = bf16[128,2048]{1,0:T(8,128)(2,1)} collective-permute-done((bf16[128,2048]{1,0:T(8,128)(2,1)S(1)}, bf16[128,2048]{1,0:T(8,128)(2,1)}, u32[]{:S(2)}, u32[]{:S(2)}) %collective-permute-start.46) | collective-permute-done | bytes 524320 | tf_op jit(solution)/shard_map/ppermute | solution.py:175
  400.3 7.4 %collective-permute-done.59 = bf16[128,2048]{1,0:T(8,128)(2,1)S(1)} collective-permute-done((bf16[128,2048]{1,0:T(8,128)(2,1)S(1)}, bf16[128,2048]{1,0:T(8,128)(2,1)S(1)}, u32[]{:S(2)}, u32[]{:S(2)}) %collective-permute-start.59) | collective-permute-done | bytes 524320 | tf_op jit(solution)/shard_map/ppermute | solution.py:175
  412.8 5.1 fusion.14
  417.9 5.3 multiply_reduce_fusion
  449.7 2.8 collective-permute-done.90
  452.5 5.3 collective-permute-start.67
  460.4 4.3 collective-permute-start.68
  468.0 9.4 %collective-permute-start.69 = (bf16[128,256]{1,0:T(8,128)(2,1)S(1)}, bf16[128,256]{1,0:T(8,128)(2,1)S(1)}, u32[]{:S(2)}, u32[]{:S(2)}) collective-permute-start(bf16[128,256]{1,0:T(8,128)(2,1)S(1)} %get-tuple-element.110), channel_id=1, source_target_pairs={{0,1},{1,2},{2,3},{4,5},{5,6},{6,7},{8,9},{9,10},{10,11},{12,13},{... | collective-permute-start | bytes 196616 | tf_op jit(solution)/shard_map/ppermute | solution.py:159
  478.7 4.3 add_convert_fusion
  483.6 4.2 collective-permute-start.60
  488.1 6.4 collective-permute-done.112
  494.5 5.3 collective-permute-start.91
  499.9 4.1 add_convert_fusion.2
  506.4 3.9 collective-permute-done.94
  518.6 4.8 collective-permute-done.96
  529.5 3.5 collective-permute-done.61
  534.9 6.8 collective-permute-done.86
  543.4 3.2 collective-permute-done.99
  548.4 9.5 %collective-permute-start.62 = (bf16[128,2048]{1,0:T(8,128)(2,1)S(1)}, bf16[128,2048]{1,0:T(8,128)(2,1)S(1)}, u32[]{:S(2)}, u32[]{:S(2)}) collective-permute-start(bf16[128,2048]{1,0:T(8,128)(2,1)S(1)} %get-tuple-element.94), channel_id=1, source_target_pairs={{0,1},{1,2},{2,3},{4,5},{5,6},{6,7},{8,9},{9,10},{10,11},{12,13},{... | collective-permute-start | bytes 1572872 | tf_op jit(solution)/shard_map/ppermute | solution.py:159
  562.7 64.1 %collective-permute-done.100 = bf16[512,256]{1,0:T(8,128)(2,1)S(1)} collective-permute-done((bf16[512,256]{1,0:T(8,128)(2,1)S(1)}, bf16[512,256]{1,0:T(8,128)(2,1)S(1)}, u32[]{:S(2)}, u32[]{:S(2)}) %collective-permute-start.100) | collective-permute-done | bytes 262176 | tf_op jit(solution)/shard_map/ppermute | solution.py:76
  630.6 3.8 collective-permute-done.79
  646.7 4.3 collective-permute-done.87
  658.7 7.0 %collective-permute-done.76 = bf16[128,2048]{1,0:T(8,128)(2,1)S(1)} collective-permute-done((bf16[128,2048]{1,0:T(8,128)(2,1)S(1)}, bf16[128,2048]{1,0:T(8,128)(2,1)S(1)}, u32[]{:S(2)}, u32[]{:S(2)}) %collective-permute-start.76) | collective-permute-done | bytes 524320 | tf_op jit(solution)/shard_map/ppermute | solution.py:175
  667.7 2.8 convert_add_fusion.1
  670.5 7.8 %collective-permute-done.77 = bf16[128,2048]{1,0:T(8,128)(2,1)S(1)} collective-permute-done((bf16[128,2048]{1,0:T(8,128)(2,1)S(1)}, bf16[128,2048]{1,0:T(8,128)(2,1)S(1)}, u32[]{:S(2)}, u32[]{:S(2)}) %collective-permute-start.77) | collective-permute-done | bytes 524320 | tf_op jit(solution)/shard_map/ppermute | solution.py:175
  679.9 10.1 %collective-permute-done.78 = bf16[128,2048]{1,0:T(8,128)(2,1)S(1)} collective-permute-done((bf16[128,2048]{1,0:T(8,128)(2,1)S(1)}, bf16[128,2048]{1,0:T(8,128)(2,1)S(1)}, u32[]{:S(2)}, u32[]{:S(2)}) %collective-permute-start.78) | collective-permute-done | bytes 524320 | tf_op jit(solution)/shard_map/ppermute | solution.py:175
  (594 shorter events, 270.4 us)
Async XLA Ops:
  10.2 44.6 %collective-permute-start.12 = (bf16[512,512]{1,0:T(8,128)(2,1)}, bf16[512,512]{1,0:T(8,128)(2,1)}, u32[]{:S(2)}, u32[]{:S(2)}) collective-permute-start(bf16[512,512]{1,0:T(8,128)(2,1)} %param.26), channel_id=1, source_target_pairs={{0,8},{8,0},{16,24},{24,16},{1,9},{9,1},{17,25},{25,17},{2,10},{10... | collective-permute-start | bytes 1572872 | tf_op jit(solution)/shard_map/ppermute | solution.py:76
  10.4 46.4 %collective-permute-start.3 = (bf16[512,512]{1,0:T(8,128)(2,1)}, bf16[512,512]{1,0:T(8,128)(2,1)}, u32[]{:S(2)}, u32[]{:S(2)}) collective-permute-start(bf16[512,512]{1,0:T(8,128)(2,1)} %param.22), channel_id=1, source_target_pairs={{0,8},{8,0},{16,24},{24,16},{1,9},{9,1},{17,25},{25,17},{2,10},{10... | collective-permute-start | bytes 1572872 | tf_op jit(solution)/shard_map/ppermute | solution.py:76
  10.7 28.4 %collective-permute-start.7 = (bf16[512,256]{1,0:T(8,128)(2,1)}, bf16[512,256]{1,0:T(8,128)(2,1)}, u32[]{:S(2)}, u32[]{:S(2)}) collective-permute-start(bf16[512,256]{1,0:T(8,128)(2,1)} %param.24), channel_id=1, source_target_pairs={{0,8},{8,0},{16,24},{24,16},{1,9},{9,1},{17,25},{25,17},{2,10},{10... | collective-permute-start | bytes 786440 | tf_op jit(solution)/shard_map/ppermute | solution.py:76
  20.6 18.4 %collective-permute-start.4 = (bf16[256,512]{1,0:T(8,128)(2,1)}, bf16[256,512]{1,0:T(8,128)(2,1)}, u32[]{:S(2)}, u32[]{:S(2)}) collective-permute-start(bf16[256,512]{1,0:T(8,128)(2,1)} %constant_dynamic-slice_fusion.6), channel_id=1, source_target_pairs={{0,16},{8,24},{16,0},{24,8},{1,17},{9,25},{17,1},{25,9},{2,18},{10... | collective-permute-start | bytes 786440 | tf_op jit(solution)/shard_map/ppermute | solution.py:76
  54.8 20.4 %collective-permute-start.15 = (bf16[512,512]{1,0:T(8,128)(2,1)}, bf16[512,512]{1,0:T(8,128)(2,1)}, u32[]{:S(2)}, u32[]{:S(2)}) collective-permute-start(bf16[512,512]{1,0:T(8,128)(2,1)} %constant_dynamic-update-slice_fusion.49), channel_id=1, source_target_pairs={{0,8},{8,0},{16,24},{24,16},{1,9},{9,1},{17,25},{25,17},{2,10},{10... | collective-permute-start | bytes 1572872 | tf_op jit(solution)/shard_map/ppermute | solution.py:76
  82.6 15.6 %collective-permute-start.16 = (bf16[128,2048]{1,0:T(8,128)(2,1)}, bf16[128,2048]{1,0:T(8,128)(2,1)}, u32[]{:S(2)}, u32[]{:S(2)}) collective-permute-start(bf16[128,2048]{1,0:T(8,128)(2,1)} %get-tuple-element.108), channel_id=1, source_target_pairs={{0,1},{4,5},{8,9},{12,13},{16,17},{20,21},{24,25},{28,29}} | collective-permute-start | bytes 1572872 | tf_op jit(solution)/shard_map/ppermute | solution.py:159
  86.9 78.6 %collective-permute-start.28 = (bf16[512,2048]{1,0:T(8,128)(2,1)}, bf16[512,2048]{1,0:T(8,128)(2,1)}, u32[]{:S(2)}, u32[]{:S(2)}) collective-permute-start(bf16[512,2048]{1,0:T(8,128)(2,1)} %param.30), channel_id=1, source_target_pairs={{0,8},{8,0},{16,24},{24,16},{1,9},{9,1},{17,25},{25,17},{2,10},{10... | collective-permute-start | bytes 6291464 | tf_op jit(solution)/shard_map/ppermute | solution.py:76
  89.4 26.2 %collective-permute-start.29 = (bf16[256,2048]{1,0:T(8,128)(2,1)}, bf16[256,2048]{1,0:T(8,128)(2,1)S(1)}, u32[]{:S(2)}, u32[]{:S(2)}) collective-permute-start(bf16[256,2048]{1,0:T(8,128)(2,1)} %constant_dynamic-slice_fusion.3), channel_id=1, source_target_pairs={{0,16},{8,24},{16,0},{24,8},{1,17},{9,25},{17,1},{25,9},{2,18},{10... | collective-permute-start | bytes 3145736 | tf_op jit(solution)/shard_map/ppermute | solution.py:76
  92.2 45.4 %collective-permute-start.33 = (bf16[1024,512]{1,0:T(8,128)(2,1)}, bf16[1024,512]{1,0:T(8,128)(2,1)}, u32[]{:S(2)}, u32[]{:S(2)}) collective-permute-start(bf16[1024,512]{1,0:T(8,128)(2,1)} %constant_dynamic-slice_fusion.2), channel_id=1, source_target_pairs={{0,16},{8,24},{16,0},{24,8},{1,17},{9,25},{17,1},{25,9},{2,18},{10... | collective-permute-start | bytes 3145736 | tf_op jit(solution)/shard_map/ppermute | solution.py:76
  93.7 23.4 %collective-permute-start.19 = (bf16[128,2048]{1,0:T(8,128)(2,1)}, bf16[128,2048]{1,0:T(8,128)(2,1)}, u32[]{:S(2)}, u32[]{:S(2)}) collective-permute-start(bf16[128,2048]{1,0:T(8,128)(2,1)} %get-tuple-element.109), channel_id=1, source_target_pairs={{3,2},{7,6},{11,10},{15,14},{19,18},{23,22},{27,26},{31,30}} | collective-permute-start | bytes 1572872 | tf_op jit(solution)/shard_map/ppermute | solution.py:164
  100.3 16.8 %collective-permute-start.17 = (bf16[128,2048]{1,0:T(8,128)(2,1)}, bf16[128,2048]{1,0:T(8,128)(2,1)}, u32[]{:S(2)}, u32[]{:S(2)}) collective-permute-start(bf16[128,2048]{1,0:T(8,128)(2,1)} %fusion.56), channel_id=1, source_target_pairs={{0,1},{1,2},{4,5},{5,6},{8,9},{9,10},{12,13},{13,14},{16,17},{17,1... | collective-permute-start | bytes 1572872 | tf_op jit(solution)/shard_map/ppermute | solution.py:159
  115.6 31.8 %collective-permute-start.30 = (bf16[256,2048]{1,0:T(8,128)(2,1)S(1)}, bf16[256,2048]{1,0:T(8,128)(2,1)}, u32[]{:S(2)}, u32[]{:S(2)}) collective-permute-start(bf16[256,2048]{1,0:T(8,128)(2,1)S(1)} %collective-permute-done.29), channel_id=1, source_target_pairs={{0,4},{4,0},{1,5},{5,1},{2,6},{6,2},{3,7},{7,3},{8,12},{12,8},{9,1... | collective-permute-start | bytes 3145736 | tf_op jit(solution)/shard_map/ppermute | solution.py:76
  119.7 23.6 %collective-permute-start.20 = (bf16[128,2048]{1,0:T(8,128)(2,1)}, bf16[128,2048]{1,0:T(8,128)(2,1)}, u32[]{:S(2)}, u32[]{:S(2)}) collective-permute-start(bf16[128,2048]{1,0:T(8,128)(2,1)} %get-tuple-element.107), channel_id=1, source_target_pairs={{3,2},{2,1},{7,6},{6,5},{11,10},{10,9},{15,14},{14,13},{19,18},{18... | collective-permute-start | bytes 1572872 | tf_op jit(solution)/shard_map/ppermute | solution.py:164
  137.6 24.8 %collective-permute-start.34 = (bf16[1024,512]{1,0:T(8,128)(2,1)}, bf16[1024,512]{1,0:T(8,128)(2,1)S(1)}, u32[]{:S(2)}, u32[]{:S(2)}) collective-permute-start(bf16[1024,512]{1,0:T(8,128)(2,1)} %collective-permute-done.33), channel_id=1, source_target_pairs={{0,4},{4,0},{1,5},{5,1},{2,6},{6,2},{3,7},{7,3},{8,12},{12,8},{9,1... | collective-permute-start | bytes 3145736 | tf_op jit(solution)/shard_map/ppermute | solution.py:76
  141.7 20.7 %collective-permute-start.18 = (bf16[128,2048]{1,0:T(8,128)(2,1)S(1)}, bf16[128,2048]{1,0:T(8,128)(2,1)S(1)}, u32[]{:S(2)}, u32[]{:S(2)}) collective-permute-start(bf16[128,2048]{1,0:T(8,128)(2,1)S(1)} %copy-done.56), channel_id=1, source_target_pairs={{0,1},{1,2},{2,3},{4,5},{5,6},{6,7},{8,9},{9,10},{10,11},{12,13},{... | collective-permute-start | bytes 1572872 | tf_op jit(solution)/shard_map/ppermute | solution.py:159
  144.6 18.4 %collective-permute-start.21 = (bf16[128,2048]{1,0:T(8,128)(2,1)S(1)}, bf16[128,2048]{1,0:T(8,128)(2,1)S(1)}, u32[]{:S(2)}, u32[]{:S(2)}) collective-permute-start(bf16[128,2048]{1,0:T(8,128)(2,1)S(1)} %fusion.55), channel_id=1, source_target_pairs={{3,2},{2,1},{1,0},{7,6},{6,5},{5,4},{11,10},{10,9},{9,8},{15,14},{... | collective-permute-start | bytes 1572872 | tf_op jit(solution)/shard_map/ppermute | solution.py:164
  147.4 30.4 %collective-permute-start.32 = (bf16[2048,512]{1,0:T(8,128)(2,1)S(1)}, bf16[2048,512]{1,0:T(8,128)(2,1)S(1)}, u32[]{:S(2)}, u32[]{:S(2)}) collective-permute-start(bf16[2048,512]{1,0:T(8,128)(2,1)S(1)} %copy-done.11), channel_id=1, source_target_pairs={{0,8},{8,0},{16,24},{24,16},{1,9},{9,1},{17,25},{25,17},{2,10},{10... | collective-permute-start | bytes 6291464 | tf_op jit(solution)/shard_map/ppermute | solution.py:76
  162.3 39.2 %collective-permute-start.31 = (bf16[512,2048]{1,0:T(8,128)(2,1)}, bf16[512,2048]{1,0:T(8,128)(2,1)}, u32[]{:S(2)}, u32[]{:S(2)}) collective-permute-start(bf16[512,2048]{1,0:T(8,128)(2,1)} %constant_dynamic-update-slice_fusion.43), channel_id=1, source_target_pairs={{0,8},{8,0},{16,24},{24,16},{1,9},{9,1},{17,25},{25,17},{2,10},{10... | collective-permute-start | bytes 6291464 | tf_op jit(solution)/shard_map/ppermute | solution.py:76
  162.4 25.4 %collective-permute-start.35 = (bf16[2048,512]{1,0:T(8,128)(2,1)S(1)}, bf16[2048,512]{1,0:T(8,128)(2,1)S(1)}, u32[]{:S(2)}, u32[]{:S(2)}) collective-permute-start(bf16[2048,512]{1,0:T(8,128)(2,1)S(1)} %constant_dynamic-update-slice_fusion.37), channel_id=1, source_target_pairs={{0,8},{8,0},{16,24},{24,16},{1,9},{9,1},{17,25},{25,17},{2,10},{10... | collective-permute-start | bytes 6291464 | tf_op jit(solution)/shard_map/ppermute | solution.py:76
  169.3 15.8 %collective-permute-start.25 = (bf16[128,2048]{1,0:T(8,128)(2,1)S(1)}, bf16[128,2048]{1,0:T(8,128)(2,1)S(1)}, u32[]{:S(2)}, u32[]{:S(2)}) collective-permute-start(bf16[128,2048]{1,0:T(8,128)(2,1)S(1)} %add_convert_fusion.8), channel_id=1, source_target_pairs={{3,2},{2,1},{1,0},{7,6},{6,5},{5,4},{11,10},{10,9},{9,8},{15,14},{... | collective-permute-start | bytes 1572872 | tf_op jit(solution)/shard_map/ppermute | solution.py:175
  185.0 15.0 %collective-permute-start.26 = (bf16[128,2048]{1,0:T(8,128)(2,1)S(1)}, bf16[128,2048]{1,0:T(8,128)(2,1)}, u32[]{:S(2)}, u32[]{:S(2)}) collective-permute-start(bf16[128,2048]{1,0:T(8,128)(2,1)S(1)} %collective-permute-done.25), channel_id=1, source_target_pairs={{2,1},{1,0},{6,5},{5,4},{10,9},{9,8},{14,13},{13,12},{18,17},{17,1... | collective-permute-start | bytes 1572872 | tf_op jit(solution)/shard_map/ppermute | solution.py:175
  186.3 17.1 %collective-permute-start.24 = (bf16[128,2048]{1,0:T(8,128)(2,1)S(1)}, bf16[128,2048]{1,0:T(8,128)(2,1)}, u32[]{:S(2)}, u32[]{:S(2)}) collective-permute-start(bf16[128,2048]{1,0:T(8,128)(2,1)S(1)} %collective-permute-done.23), channel_id=1, source_target_pairs={{2,3},{6,7},{10,11},{14,15},{18,19},{22,23},{26,27},{30,31}} | collective-permute-start | bytes 1572872 | tf_op jit(solution)/shard_map/ppermute | solution.py:174
  238.8 17.8 %collective-permute-start.36 = (bf16[128,2048]{1,0:T(8,128)(2,1)S(1)}, bf16[128,2048]{1,0:T(8,128)(2,1)S(1)}, u32[]{:S(2)}, u32[]{:S(2)}) collective-permute-start(bf16[128,2048]{1,0:T(8,128)(2,1)S(1)} %get-tuple-element.104), channel_id=1, source_target_pairs={{0,1},{4,5},{8,9},{12,13},{16,17},{20,21},{24,25},{28,29}} | collective-permute-start | bytes 1572872 | tf_op jit(solution)/shard_map/ppermute | solution.py:159
  240.1 25.1 %collective-permute-start.51 = (bf16[128,2048]{1,0:T(8,128)(2,1)}, bf16[128,2048]{1,0:T(8,128)(2,1)}, u32[]{:S(2)}, u32[]{:S(2)}) collective-permute-start(bf16[128,2048]{1,0:T(8,128)(2,1)} %get-tuple-element.101), channel_id=1, source_target_pairs={{3,2},{7,6},{11,10},{15,14},{19,18},{23,22},{27,26},{31,30}} | collective-permute-start | bytes 1572872 | tf_op jit(solution)/shard_map/ppermute | solution.py:164
  241.5 28.8 %collective-permute-start.39 = (bf16[128,2048]{1,0:T(8,128)(2,1)}, bf16[128,2048]{1,0:T(8,128)(2,1)}, u32[]{:S(2)}, u32[]{:S(2)}) collective-permute-start(bf16[128,2048]{1,0:T(8,128)(2,1)} %get-tuple-element.105), channel_id=1, source_target_pairs={{3,2},{7,6},{11,10},{15,14},{19,18},{23,22},{27,26},{31,30}} | collective-permute-start | bytes 1572872 | tf_op jit(solution)/shard_map/ppermute | solution.py:164
  246.2 21.6 %collective-permute-start.49 = (bf16[128,2048]{1,0:T(8,128)(2,1)}, bf16[128,2048]{1,0:T(8,128)(2,1)}, u32[]{:S(2)}, u32[]{:S(2)}) collective-permute-start(bf16[128,2048]{1,0:T(8,128)(2,1)} %fusion.45), channel_id=1, source_target_pairs={{0,1},{1,2},{4,5},{5,6},{8,9},{9,10},{12,13},{13,14},{16,17},{17,1... | collective-permute-start | bytes 1572872 | tf_op jit(solution)/shard_map/ppermute | solution.py:159
  257.5 18.0 %collective-permute-start.37 = (bf16[128,2048]{1,0:T(8,128)(2,1)}, bf16[128,2048]{1,0:T(8,128)(2,1)}, u32[]{:S(2)}, u32[]{:S(2)}) collective-permute-start(bf16[128,2048]{1,0:T(8,128)(2,1)} %fusion.50), channel_id=1, source_target_pairs={{0,1},{1,2},{4,5},{5,6},{8,9},{9,10},{12,13},{13,14},{16,17},{17,1... | collective-permute-start | bytes 1572872 | tf_op jit(solution)/shard_map/ppermute | solution.py:159
  269.5 17.8 %collective-permute-start.52 = (bf16[128,2048]{1,0:T(8,128)(2,1)S(1)}, bf16[128,2048]{1,0:T(8,128)(2,1)S(1)}, u32[]{:S(2)}, u32[]{:S(2)}) collective-permute-start(bf16[128,2048]{1,0:T(8,128)(2,1)S(1)} %get-tuple-element.99), channel_id=1, source_target_pairs={{3,2},{2,1},{7,6},{6,5},{11,10},{10,9},{15,14},{14,13},{19,18},{18... | collective-permute-start | bytes 1572872 | tf_op jit(solution)/shard_map/ppermute | solution.py:164
  277.7 20.7 %collective-permute-start.50 = (bf16[128,2048]{1,0:T(8,128)(2,1)S(1)}, bf16[128,2048]{1,0:T(8,128)(2,1)S(1)}, u32[]{:S(2)}, u32[]{:S(2)}) collective-permute-start(bf16[128,2048]{1,0:T(8,128)(2,1)S(1)} %get-tuple-element.98), channel_id=1, source_target_pairs={{0,1},{1,2},{2,3},{4,5},{5,6},{6,7},{8,9},{9,10},{10,11},{12,13},{... | collective-permute-start | bytes 1572872 | tf_op jit(solution)/shard_map/ppermute | solution.py:159
  282.8 19.0 %collective-permute-start.38 = (bf16[128,2048]{1,0:T(8,128)(2,1)S(1)}, bf16[128,2048]{1,0:T(8,128)(2,1)S(1)}, u32[]{:S(2)}, u32[]{:S(2)}) collective-permute-start(bf16[128,2048]{1,0:T(8,128)(2,1)S(1)} %get-tuple-element.102), channel_id=1, source_target_pairs={{0,1},{1,2},{2,3},{4,5},{5,6},{6,7},{8,9},{9,10},{10,11},{12,13},{... | collective-permute-start | bytes 1572872 | tf_op jit(solution)/shard_map/ppermute | solution.py:159
  287.5 15.2 %collective-permute-start.53 = (bf16[128,2048]{1,0:T(8,128)(2,1)S(1)}, bf16[128,2048]{1,0:T(8,128)(2,1)S(1)}, u32[]{:S(2)}, u32[]{:S(2)}) collective-permute-start(bf16[128,2048]{1,0:T(8,128)(2,1)S(1)} %fusion.44), channel_id=1, source_target_pairs={{3,2},{2,1},{1,0},{7,6},{6,5},{5,4},{11,10},{10,9},{9,8},{15,14},{... | collective-permute-start | bytes 1572872 | tf_op jit(solution)/shard_map/ppermute | solution.py:164
  288.9 21.1 %collective-permute-start.41 = (bf16[128,2048]{1,0:T(8,128)(2,1)S(1)}, bf16[128,2048]{1,0:T(8,128)(2,1)S(1)}, u32[]{:S(2)}, u32[]{:S(2)}) collective-permute-start(bf16[128,2048]{1,0:T(8,128)(2,1)S(1)} %fusion.49), channel_id=1, source_target_pairs={{3,2},{2,1},{1,0},{7,6},{6,5},{5,4},{11,10},{10,9},{9,8},{15,14},{... | collective-permute-start | bytes 1572872 | tf_op jit(solution)/shard_map/ppermute | solution.py:164
  294.5 56.0 %collective-permute-start.115 = (bf16[2048,512]{1,0:T(8,128)(2,1)}, bf16[2048,512]{1,0:T(8,128)(2,1)}, u32[]{:S(2)}, u32[]{:S(2)}) collective-permute-start(bf16[2048,512]{1,0:T(8,128)(2,1)} %convolution_convert_fusion), channel_id=1, source_target_pairs={{0,8},{8,0},{16,24},{24,16},{1,9},{9,1},{17,25},{25,17},{2,10},{10... | collective-permute-start | bytes 6291464 | tf_op jit(solution)/shard_map/ppermute | solution.py:76
  298.4 58.2 %collective-permute-start.111 = (bf16[512,2048]{1,0:T(8,128)(2,1)}, bf16[512,2048]{1,0:T(8,128)(2,1)}, u32[]{:S(2)}, u32[]{:S(2)}) collective-permute-start(bf16[512,2048]{1,0:T(8,128)(2,1)} %convolution_convert_fusion.2), channel_id=1, source_target_pairs={{0,8},{8,0},{16,24},{24,16},{1,9},{9,1},{17,25},{25,17},{2,10},{10... | collective-permute-start | bytes 6291464 | tf_op jit(solution)/shard_map/ppermute | solution.py:76
  337.1 21.1 %collective-permute-start.57 = (bf16[128,2048]{1,0:T(8,128)(2,1)S(1)}, bf16[128,2048]{1,0:T(8,128)(2,1)S(1)}, u32[]{:S(2)}, u32[]{:S(2)}) collective-permute-start(bf16[128,2048]{1,0:T(8,128)(2,1)S(1)} %copy-done.28), channel_id=1, source_target_pairs={{3,2},{2,1},{1,0},{7,6},{6,5},{5,4},{11,10},{10,9},{9,8},{15,14},{... | collective-permute-start | bytes 1572872 | tf_op jit(solution)/shard_map/ppermute | solution.py:175
  338.7 20.8 %collective-permute-start.55 = (bf16[128,2048]{1,0:T(8,128)(2,1)S(1)}, bf16[128,2048]{1,0:T(8,128)(2,1)S(1)}, u32[]{:S(2)}, u32[]{:S(2)}) collective-permute-start(bf16[128,2048]{1,0:T(8,128)(2,1)S(1)} %collective-permute-done.54), channel_id=1, source_target_pairs={{1,2},{2,3},{5,6},{6,7},{9,10},{10,11},{13,14},{14,15},{17,18},{18... | collective-permute-start | bytes 1572872 | tf_op jit(solution)/shard_map/ppermute | solution.py:174
  343.3 26.1 %collective-permute-start.42 = (bf16[128,2048]{1,0:T(8,128)(2,1)S(1)}, bf16[128,2048]{1,0:T(8,128)(2,1)S(1)}, u32[]{:S(2)}, u32[]{:S(2)}) collective-permute-start(bf16[128,2048]{1,0:T(8,128)(2,1)S(1)} %copy-done.39), channel_id=1, source_target_pairs={{0,1},{1,2},{2,3},{4,5},{5,6},{6,7},{8,9},{9,10},{10,11},{12,13},{... | collective-permute-start | bytes 1572872 | tf_op jit(solution)/shard_map/ppermute | solution.py:174
  355.4 16.7 %collective-permute-start.45 = (bf16[128,2048]{1,0:T(8,128)(2,1)S(1)}, bf16[128,2048]{1,0:T(8,128)(2,1)S(1)}, u32[]{:S(2)}, u32[]{:S(2)}) collective-permute-start(bf16[128,2048]{1,0:T(8,128)(2,1)S(1)} %copy-done.39), channel_id=1, source_target_pairs={{3,2},{2,1},{1,0},{7,6},{6,5},{5,4},{11,10},{10,9},{9,8},{15,14},{... | collective-permute-start | bytes 1572872 | tf_op jit(solution)/shard_map/ppermute | solution.py:175
  358.2 23.8 %collective-permute-start.58 = (bf16[128,2048]{1,0:T(8,128)(2,1)S(1)}, bf16[128,2048]{1,0:T(8,128)(2,1)S(1)}, u32[]{:S(2)}, u32[]{:S(2)}) collective-permute-start(bf16[128,2048]{1,0:T(8,128)(2,1)S(1)} %collective-permute-done.57), channel_id=1, source_target_pairs={{2,1},{1,0},{6,5},{5,4},{10,9},{9,8},{14,13},{13,12},{18,17},{17,1... | collective-permute-start | bytes 1572872 | tf_op jit(solution)/shard_map/ppermute | solution.py:175
  359.5 23.8 %collective-permute-start.56 = (bf16[128,2048]{1,0:T(8,128)(2,1)S(1)}, bf16[128,2048]{1,0:T(8,128)(2,1)S(1)}, u32[]{:S(2)}, u32[]{:S(2)}) collective-permute-start(bf16[128,2048]{1,0:T(8,128)(2,1)S(1)} %collective-permute-done.55), channel_id=1, source_target_pairs={{2,3},{6,7},{10,11},{14,15},{18,19},{22,23},{26,27},{30,31}} | collective-permute-start | bytes 1572872 | tf_op jit(solution)/shard_map/ppermute | solution.py:174
  365.0 102.9 %collective-permute-start.114 = (bf16[2048,512]{1,0:T(8,128)(2,1)}, bf16[2048,512]{1,0:T(8,128)(2,1)}, u32[]{:S(2)}, u32[]{:S(2)}) collective-permute-start(bf16[2048,512]{1,0:T(8,128)(2,1)} %convolution_convert_fusion.1), channel_id=1, source_target_pairs={{0,8},{8,0},{16,24},{24,16},{1,9},{9,1},{17,25},{25,17},{2,10},{10... | collective-permute-start | bytes 6291464 | tf_op jit(solution)/shard_map/ppermute | solution.py:76
  369.4 118.4 %collective-permute-start.110 = (bf16[512,2048]{1,0:T(8,128)(2,1)}, bf16[512,2048]{1,0:T(8,128)(2,1)}, u32[]{:S(2)}, u32[]{:S(2)}) collective-permute-start(bf16[512,2048]{1,0:T(8,128)(2,1)} %convolution_convert_fusion.3), channel_id=1, source_target_pairs={{0,8},{8,0},{16,24},{24,16},{1,9},{9,1},{17,25},{25,17},{2,10},{10... | collective-permute-start | bytes 6291464 | tf_op jit(solution)/shard_map/ppermute | solution.py:76
  382.0 16.8 %collective-permute-start.46 = (bf16[128,2048]{1,0:T(8,128)(2,1)S(1)}, bf16[128,2048]{1,0:T(8,128)(2,1)}, u32[]{:S(2)}, u32[]{:S(2)}) collective-permute-start(bf16[128,2048]{1,0:T(8,128)(2,1)S(1)} %collective-permute-done.45), channel_id=1, source_target_pairs={{2,1},{1,0},{6,5},{5,4},{10,9},{9,8},{14,13},{13,12},{18,17},{17,1... | collective-permute-start | bytes 1572872 | tf_op jit(solution)/shard_map/ppermute | solution.py:175
  383.3 24.4 %collective-permute-start.59 = (bf16[128,2048]{1,0:T(8,128)(2,1)S(1)}, bf16[128,2048]{1,0:T(8,128)(2,1)S(1)}, u32[]{:S(2)}, u32[]{:S(2)}) collective-permute-start(bf16[128,2048]{1,0:T(8,128)(2,1)S(1)} %collective-permute-done.58), channel_id=1, source_target_pairs={{1,0},{5,4},{9,8},{13,12},{17,16},{21,20},{25,24},{29,28}} | collective-permute-start | bytes 1572872 | tf_op jit(solution)/shard_map/ppermute | solution.py:175
  384.9 92.5 %collective-permute-start.116 = (bf16[2048,512]{1,0:T(8,128)(2,1)}, bf16[2048,512]{1,0:T(8,128)(2,1)}, u32[]{:S(2)}, u32[]{:S(2)}) collective-permute-start(bf16[2048,512]{1,0:T(8,128)(2,1)} %add_convert_fusion.1), channel_id=1, source_target_pairs={{0,16},{8,24},{16,0},{24,8},{1,17},{9,25},{17,1},{25,9},{2,18},{10... | collective-permute-start | bytes 6291464 | tf_op jit(solution)/shard_map/ppermute | solution.py:76
  398.8 34.5 %collective-permute-start.44 = (bf16[128,2048]{1,0:T(8,128)(2,1)}, bf16[128,2048]{1,0:T(8,128)(2,1)}, u32[]{:S(2)}, u32[]{:S(2)}) collective-permute-start(bf16[128,2048]{1,0:T(8,128)(2,1)} %collective-permute-done.43), channel_id=1, source_target_pairs={{2,3},{6,7},{10,11},{14,15},{18,19},{22,23},{26,27},{30,31}} | collective-permute-start | bytes 1572872 | tf_op jit(solution)/shard_map/ppermute | solution.py:174
  407.7 31.9 %collective-permute-start.47 = (bf16[128,2048]{1,0:T(8,128)(2,1)}, bf16[128,2048]{1,0:T(8,128)(2,1)}, u32[]{:S(2)}, u32[]{:S(2)}) collective-permute-start(bf16[128,2048]{1,0:T(8,128)(2,1)} %collective-permute-done.46), channel_id=1, source_target_pairs={{1,0},{5,4},{9,8},{13,12},{17,16},{21,20},{25,24},{29,28}} | collective-permute-start | bytes 1572872 | tf_op jit(solution)/shard_map/ppermute | solution.py:175
  433.4 15.5 %collective-permute-start.66 = (bf16[1,512,256]{1,2,0:T(8,128)(2,1)S(1)}, bf16[1,512,256]{1,2,0:T(8,128)(2,1)S(1)}, u32[]{:S(2)}, u32[]{:S(2)}) collective-permute-start(bf16[1,512,256]{1,2,0:T(8,128)(2,1)S(1)} %fusion.95), channel_id=1, source_target_pairs={{0,4},{4,0},{1,5},{5,1},{2,6},{6,2},{3,7},{7,3},{8,12},{12,8},{9,1... | collective-permute-start | bytes 786440 | tf_op jit(solution)/shard_map/ppermute | solution.py:330
  447.3 47.2 %collective-permute-start.112 = (bf16[512,2048]{1,0:T(8,128)(2,1)}, bf16[512,2048]{1,0:T(8,128)(2,1)}, u32[]{:S(2)}, u32[]{:S(2)}) collective-permute-start(bf16[512,2048]{1,0:T(8,128)(2,1)} %add_convert_fusion.3), channel_id=1, source_target_pairs={{0,16},{8,24},{16,0},{24,8},{1,17},{9,25},{17,1},{25,9},{2,18},{10... | collective-permute-start | bytes 6291464 | tf_op jit(solution)/shard_map/ppermute | solution.py:76
  467.9 90.1 %collective-permute-start.101 = (bf16[512,512]{1,0:T(8,128)(2,1)}, bf16[512,512]{1,0:T(8,128)(2,1)S(1)}, u32[]{:S(2)}, u32[]{:S(2)}) collective-permute-start(bf16[512,512]{1,0:T(8,128)(2,1)} %convolution_convert_fusion.10), channel_id=1, source_target_pairs={{0,8},{8,0},{16,24},{24,16},{1,9},{9,1},{17,25},{25,17},{2,10},{10... | collective-permute-start | bytes 1572872 | tf_op jit(solution)/shard_map/ppermute | solution.py:76
  468.0 15.1 %collective-permute-start.69 = (bf16[128,256]{1,0:T(8,128)(2,1)S(1)}, bf16[128,256]{1,0:T(8,128)(2,1)S(1)}, u32[]{:S(2)}, u32[]{:S(2)}) collective-permute-start(bf16[128,256]{1,0:T(8,128)(2,1)S(1)} %get-tuple-element.110), channel_id=1, source_target_pairs={{0,1},{1,2},{2,3},{4,5},{5,6},{6,7},{8,9},{9,10},{10,11},{12,13},{... | collective-permute-start | bytes 196616 | tf_op jit(solution)/shard_map/ppermute | solution.py:159
  483.1 23.2 %collective-permute-start.102 = (bf16[512,512]{1,0:T(8,128)(2,1)S(1)}, bf16[512,512]{1,0:T(8,128)(2,1)S(1)}, u32[]{:S(2)}, u32[]{:S(2)}) collective-permute-start(bf16[512,512]{1,0:T(8,128)(2,1)S(1)} %copy-done.72), channel_id=1, source_target_pairs={{0,8},{8,0},{16,24},{24,16},{1,9},{9,1},{17,25},{25,17},{2,10},{10... | collective-permute-start | bytes 1572872 | tf_op jit(solution)/shard_map/ppermute | solution.py:76
  483.6 20.4 %collective-permute-start.60 = (bf16[128,2048]{1,0:T(8,128)(2,1)S(1)}, bf16[128,2048]{1,0:T(8,128)(2,1)S(1)}, u32[]{:S(2)}, u32[]{:S(2)}) collective-permute-start(bf16[128,2048]{1,0:T(8,128)(2,1)S(1)} %copy-done.55), channel_id=1, source_target_pairs={{0,1},{4,5},{8,9},{12,13},{16,17},{20,21},{24,25},{28,29}} | collective-permute-start | bytes 1572872 | tf_op jit(solution)/shard_map/ppermute | solution.py:159
  487.9 37.5 %collective-permute-start.85 = (bf16[512,512]{1,0:T(8,128)(2,1)S(1)}, bf16[512,512]{1,0:T(8,128)(2,1)S(1)}, u32[]{:S(2)}, u32[]{:S(2)}) collective-permute-start(bf16[512,512]{1,0:T(8,128)(2,1)S(1)} %copy-done.71), channel_id=1, source_target_pairs={{0,8},{8,0},{16,24},{24,16},{1,9},{9,1},{17,25},{25,17},{2,10},{10... | collective-permute-start | bytes 1572872 | tf_op jit(solution)/shard_map/ppermute | solution.py:76
  506.3 27.0 %collective-permute-start.84 = (bf16[512,512]{1,0:T(8,128)(2,1)S(1)}, bf16[512,512]{1,0:T(8,128)(2,1)S(1)}, u32[]{:S(2)}, u32[]{:S(2)}) collective-permute-start(bf16[512,512]{1,0:T(8,128)(2,1)S(1)} %copy-done.70), channel_id=1, source_target_pairs={{0,8},{8,0},{16,24},{24,16},{1,9},{9,1},{17,25},{25,17},{2,10},{10... | collective-permute-start | bytes 1572872 | tf_op jit(solution)/shard_map/ppermute | solution.py:76
  527.0 14.8 %collective-permute-start.86 = (bf16[512,512]{1,0:T(8,128)(2,1)S(1)}, bf16[512,512]{1,0:T(8,128)(2,1)S(1)}, u32[]{:S(2)}, u32[]{:S(2)}) collective-permute-start(bf16[512,512]{1,0:T(8,128)(2,1)S(1)} %add_convert_fusion.6), channel_id=1, source_target_pairs={{0,16},{8,24},{16,0},{24,8},{1,17},{9,25},{17,1},{25,9},{2,18},{10... | collective-permute-start | bytes 1572872 | tf_op jit(solution)/shard_map/ppermute | solution.py:76
  528.8 127.3 %collective-permute-start.117 = (bf16[2048,512]{1,0:T(8,128)(2,1)S(1)}, bf16[2048,512]{1,0:T(8,128)(2,1)S(1)}, u32[]{:S(2)}, u32[]{:S(2)}) collective-permute-start(bf16[2048,512]{1,0:T(8,128)(2,1)S(1)} %add_convert_fusion), channel_id=1, source_target_pairs={{0,4},{4,0},{1,5},{5,1},{2,6},{6,2},{3,7},{7,3},{8,12},{12,8},{9,1... | collective-permute-start | bytes 6291464 | tf_op jit(solution)/shard_map/ppermute | solution.py:76
  542.7 125.0 %collective-permute-start.113 = (bf16[512,2048]{1,0:T(8,128)(2,1)S(1)}, bf16[512,2048]{1,0:T(8,128)(2,1)S(1)}, u32[]{:S(2)}, u32[]{:S(2)}) collective-permute-start(bf16[512,2048]{1,0:T(8,128)(2,1)S(1)} %add_convert_fusion.2), channel_id=1, source_target_pairs={{0,4},{4,0},{1,5},{5,1},{2,6},{6,2},{3,7},{7,3},{8,12},{12,8},{9,1... | collective-permute-start | bytes 6291464 | tf_op jit(solution)/shard_map/ppermute | solution.py:76
  548.4 79.9 %collective-permute-start.62 = (bf16[128,2048]{1,0:T(8,128)(2,1)S(1)}, bf16[128,2048]{1,0:T(8,128)(2,1)S(1)}, u32[]{:S(2)}, u32[]{:S(2)}) collective-permute-start(bf16[128,2048]{1,0:T(8,128)(2,1)S(1)} %get-tuple-element.94), channel_id=1, source_target_pairs={{0,1},{1,2},{2,3},{4,5},{5,6},{6,7},{8,9},{9,10},{10,11},{12,13},{... | collective-permute-start | bytes 1572872 | tf_op jit(solution)/shard_map/ppermute | solution.py:159
  558.0 68.8 %collective-permute-start.100 = (bf16[512,256]{1,0:T(8,128)(2,1)S(1)}, bf16[512,256]{1,0:T(8,128)(2,1)S(1)}, u32[]{:S(2)}, u32[]{:S(2)}) collective-permute-start(bf16[512,256]{1,0:T(8,128)(2,1)S(1)} %fusion.31), channel_id=1, source_target_pairs={{0,4},{4,0},{1,5},{5,1},{2,6},{6,2},{3,7},{7,3},{8,12},{12,8},{9,1... | collective-permute-start | bytes 786440 | tf_op jit(solution)/shard_map/ppermute | solution.py:76
  559.7 70.0 %collective-permute-start.65 = (bf16[128,2048]{1,0:T(8,128)(2,1)S(1)}, bf16[128,2048]{1,0:T(8,128)(2,1)S(1)}, u32[]{:S(2)}, u32[]{:S(2)}) collective-permute-start(bf16[128,2048]{1,0:T(8,128)(2,1)S(1)} %fusion.38), channel_id=1, source_target_pairs={{3,2},{2,1},{1,0},{7,6},{6,5},{5,4},{11,10},{10,9},{9,8},{15,14},{... | collective-permute-start | bytes 1572872 | tf_op jit(solution)/shard_map/ppermute | solution.py:164
  626.8 15.4 %collective-permute-start.104 = (bf16[512,512]{1,0:T(8,128)(2,1)S(1)}, bf16[512,512]{1,0:T(8,128)(2,1)S(1)}, u32[]{:S(2)}, u32[]{:S(2)}) collective-permute-start(bf16[512,512]{1,0:T(8,128)(2,1)S(1)} %fusion.24), channel_id=1, source_target_pairs={{0,4},{4,0},{1,5},{5,1},{2,6},{6,2},{3,7},{7,3},{8,12},{12,8},{9,1... | collective-permute-start | bytes 1572872 | tf_op jit(solution)/shard_map/ppermute | solution.py:76
  628.3 22.8 %collective-permute-start.87 = (bf16[512,512]{1,0:T(8,128)(2,1)S(1)}, bf16[512,512]{1,0:T(8,128)(2,1)S(1)}, u32[]{:S(2)}, u32[]{:S(2)}) collective-permute-start(bf16[512,512]{1,0:T(8,128)(2,1)S(1)} %add_convert_fusion.5), channel_id=1, source_target_pairs={{0,4},{4,0},{1,5},{5,1},{2,6},{6,2},{3,7},{7,3},{8,12},{12,8},{9,1... | collective-permute-start | bytes 1572872 | tf_op jit(solution)/shard_map/ppermute | solution.py:76
  640.3 15.1 %collective-permute-start.73 = (bf16[128,2048]{1,0:T(8,128)(2,1)S(1)}, bf16[128,2048]{1,0:T(8,128)(2,1)S(1)}, u32[]{:S(2)}, u32[]{:S(2)}) collective-permute-start(bf16[128,2048]{1,0:T(8,128)(2,1)S(1)} %add_convert_fusion.7), channel_id=1, source_target_pairs={{0,1},{1,2},{2,3},{4,5},{5,6},{6,7},{8,9},{9,10},{10,11},{12,13},{... | collective-permute-start | bytes 1572872 | tf_op jit(solution)/shard_map/ppermute | solution.py:174
  (140 other events, 1681.1 us)

commit v2 on v0

v2 whole, which is shorter than its diff:
```python
import functools
import math
import types

import jax
import jax.numpy as jnp
from jax import lax
from jax.experimental import pallas as pl
from jax.experimental.pallas import tpu as pltpu
from jax.sharding import PartitionSpec as P

HD = 128
EPSILON = 1e-05
NEGATIVE = -1e30
FSDP, CTX, TP = "fsdp", "ctx", "tp"
LOW, WIDE = jnp.bfloat16, jnp.float32
MESH = pl.DeviceIdType.MESH
VMEM_BYTES = 60 << 20


def flip(place, bit):
    return place + bit - 2 * bit * lax.rem(lax.div(place, bit), 2)


def bits_of(axis):
    count, bit, found = lax.axis_size(axis), 1, []
    while bit < count:
        found.append(bit)
        bit *= 2
    return found


def mm(left, right):
    return jnp.dot(left, right, preferred_element_type=WIDE)


def mm_nt(left, right):
    return lax.dot_general(left, right, (((1,), (1,)), ((), ())), preferred_element_type=WIDE)


def mm_tn(left, right):
    return lax.dot_general(left, right, (((0,), (0,)), ((), ())), preferred_element_type=WIDE)


def tiles(count, step):
    def run(work):
        def once(index, carry):
            work(pl.multiple_of(index * step, step))
            return carry

        lax.fori_loop(0, count // step, once, 0)

    return run


def norm_of(values):
    center = values - jnp.mean(values, -1, keepdims=True)
    scaled = lax.rsqrt(jnp.mean(center * center, -1, keepdims=True) + EPSILON)
    return center * scaled, scaled


def norm_backward(upstream, unit_rows, scaled, norm_gain):
    gained = upstream * norm_gain
    return scaled * (
        gained
        - jnp.mean(gained, -1, keepdims=True)
        - unit_rows * jnp.mean(gained * unit_rows, -1, keepdims=True)
    )


def send(source, target, outgo, income, axis, place):
    return pltpu.make_async_remote_copy(
        src_ref=source,
        dst_ref=target,
        send_sem=outgo,
        recv_sem=income,
        device_id={axis: place},
        device_id_type=MESH,
    )


def all_peers():
    me, place, zone = lax.axis_index(FSDP), lax.axis_index(CTX), lax.axis_index(TP)
    ctx, tp = lax.axis_size(CTX), lax.axis_size(TP)
    peers = [(FSDP, flip(me, 1)), (FSDP, flip(me, 2)), (FSDP, flip(flip(me, 1), 2))]
    peers += [(CTX, lax.rem(place + k, ctx)) for k in range(1, ctx)]
    peers += [(TP, lax.rem(zone + k, tp)) for k in range(1, tp)]
    return peers


def greet(peers):
    barrier = pltpu.get_barrier_semaphore()
    for axis, place in peers:
        pl.semaphore_signal(barrier, inc=1, device_id={axis: place}, device_id_type=MESH)
    return lambda: pl.semaphore_wait(barrier, len(peers))


def split_rows(tokens):
    rows = 32 if tokens % 512 == 0 else 16
    return rows, tokens // 2 // rows


class Line:
    def __init__(self, tokens):
        self.place, self.count = lax.axis_index(TP), lax.axis_size(TP)
        self.rows, self.chunks = split_rows(tokens)
        self.half = tokens // 2

    def at(self, half, k):
        start = half * self.half + k * self.rows
        return pl.ds(start if isinstance(start, int) else pl.multiple_of(start, self.rows), self.rows)

    def is_home(self, half):
        return self.place == (0 if half == 0 else self.count - 1)

    def is_far(self, half):
        return self.place == (self.count - 1 if half == 0 else 0)

    def toward(self, half):
        move = self.count - 1 if half == 0 else 1
        return lax.rem(self.place + move, self.count)

    def away(self, half):
        return self.toward(1 - half)


class LineSum(Line):
    def __init__(self, own, slots, sems):
        super().__init__(own.shape[0])
        self.own, self.slots = own, slots
        self.outgo, self.income = sems

    def copy(self, half, k):
        rows = self.at(half, k)
        return send(
            self.own.at[rows],
            self.slots.at[rows],
            self.outgo.at[half, k],
            self.income.at[half, k],
            TP,
            self.toward(half),
        )

    def launch(self, half, first=0, last=None):
        @pl.when(self.is_far(half))
        def _():
            for k in range(first, self.chunks if last is None else last):
                self.copy(half, k).start()

    def total(self, half, k):
        rows = self.at(half, k)
        return self.own[rows, :].astype(WIDE) + self.slots[rows, :].astype(WIDE)

    def pass_on(self, half, k):
        self.copy(half, k).wait_recv()
        self.own[self.at(half, k), :] = self.total(half, k).astype(LOW)
        self.copy(half, k).start()

    def drain(self):
        for half in range(2):

            @pl.when(jnp.logical_not(self.is_home(half)))
            def _():
                for k in range(self.chunks):
                    self.copy(half, k).wait_send()


class LineSpread(Line):
    def __init__(self, held, sems):
        super().__init__(held.shape[0])
        self.held = held
        self.outgo, self.income = sems

    def copy(self, half, k, source=None):
        rows = self.at(half, k)
        return send(
            self.held.at[rows] if source is None else source.at[rows],
            self.held.at[rows],
            self.outgo.at[half, k],
            self.income.at[half, k],
            TP,
            self.away(half),
        )

    def begin(self, half, k, source=None):
        self.copy(half, k, source).start()

    def serve(self, half, k):
        self.copy(half, k).wait_recv()

        @pl.when(jnp.logical_not(self.is_far(half)))
        def _():
            self.copy(half, k).start()

    def drain(self):
        for half in range(2):

            @pl.when(jnp.logical_not(self.is_far(half)))
            def _():
                for k in range(self.chunks):
                    self.copy(half, k).wait_send()


class Flow(Line):
    def __init__(self, line_sum, spread, home, lag):
        super().__init__(line_sum.own.shape[0])
        self.sum, self.spread, self.home, self.lag = line_sum, spread, home, lag
        self.now = 0
        self.steps = self.chunks + lag + 2 * (self.count - 1) - 1

    def launch(self, first=0, last=None):
        for half in range(2):
            self.sum.launch(half, first, last)

    def inside(self, k):
        return (k >= 0) & (k < self.chunks)

    def advance(self, count=1):
        for n in range(self.now, min(self.now + count, self.steps)):
            self.step(n)
        self.now = min(self.now + count, self.steps)

    def step(self, n):
        last = self.count - 1
        at_home = n - (last - 1)
        for half in range(2):
            hops = last - self.place if half == 0 else self.place
            k = n - (hops - 1)

            @pl.when((hops >= 1) & (hops < last) & self.inside(k))
            def _():
                self.sum.pass_on(half, k)

            if 0 <= at_home < self.chunks:

                @pl.when(self.is_home(half))
                def _():
                    self.sum.copy(half, at_home).wait_recv()
                    self.home(half, at_home)

        for half in range(2):
            hops = self.place if half == 0 else last - self.place
            k = at_home - self.lag - (hops - 1)

            @pl.when((hops >= 1) & self.inside(k))
            def _():
                self.spread.serve(half, k)

    def ready(self, chunk):
        return chunk + self.lag + 2 * (self.count - 1) - 2


class Gather:
    def __init__(self, shard, held, sems, cut):
        self.shard, self.held = shard, held
        self.me, self.place = lax.axis_index(FSDP), lax.axis_index(CTX)
        self.ctx = lax.axis_size(CTX)
        self.cut = cut
        self.rows = shard.shape[0] // self.ctx // cut
        self.near_sem, self.far_sem, self.side_sem, self.pass_sem, self.local = sems

    def part(self, place, k):
        return pl.ds(pl.multiple_of((place * self.cut + k) * self.rows, self.rows), self.rows)

    def keep(self):
        every = pl.ds(0, self.shard.shape[0])
        return pltpu.make_async_copy(self.shard, self.held(self.me, every), self.local.at[0])

    def near(self):
        every = pl.ds(0, self.shard.shape[0])
        return send(
            self.shard,
            self.held(self.me, every),
            self.near_sem.at[0],
            self.near_sem.at[1],
            FSDP,
            flip(self.me, 1),
        )

    def far(self, k):
        part = self.part(self.place, k)
        return send(
            self.shard.at[part],
            self.held(self.me, part),
            self.far_sem.at[0, k],
            self.far_sem.at[1, k],
            FSDP,
            flip(self.me, 2),
        )

    def side(self, other, k):
        held = self.held(flip(self.me, 2), self.part(self.place, k))
        return send(
            held,
            held,
            self.side_sem.at[0, other - 1, k],
            self.side_sem.at[1, other - 1, k],
            CTX,
            lax.rem(self.place + other, self.ctx),
        )

    def over(self, other, k):
        place = lax.rem(self.place + self.ctx - other, self.ctx)
        held = self.held(flip(self.me, 2), self.part(place, k))
        return send(
            held,
            held,
            self.pass_sem.at[0, other, k],
            self.pass_sem.at[1, other, k],
            FSDP,
            flip(self.me, 1),
        )

    def start(self):
        for k in range(self.cut):
            self.far(k).start()
        self.near().start()
        self.keep().start()

    def cross(self, k):
        self.far(k).wait_recv()
        for other in range(1, self.ctx):
            self.side(other, k).start()
        self.over(0, k).start()

    def pass_on(self, k):
        for other in range(1, self.ctx):
            self.side(other, k).wait_recv()
            self.over(other, k).start()

    def ready(self):
        self.keep().wait()
        self.near().wait_recv()
        for k in range(self.cut):
            for other in range(self.ctx):
                self.over(other, k).wait_recv()

    def drain(self):
        self.near().wait_send()
        for k in range(self.cut):
            self.far(k).wait_send()
            for other in range(self.ctx):
                self.over(other, k).wait_send()
                if other > 0:
                    self.side(other, k).wait_send()

    @staticmethod
    def sems(cut):
        ctx = lax.axis_size(CTX)
        shapes = ((2,), (2, cut), (2, ctx - 1, cut), (2, ctx, cut), (1,))
        return tuple(pltpu.SemaphoreType.DMA(shape) for shape in shapes)


class PieceSum:
    def __init__(self, piece, near, far, last, stages, sems, chunks):
        self.piece, self.near, self.far, self.last = piece, near, far, last
        self.stages, self.chunks = stages, chunks
        self.rows = far.shape[0] // chunks
        self.near_sem, self.far_sem, self.last_sem, self.local = sems
        self.me, self.place = lax.axis_index(FSDP), lax.axis_index(CTX)
        self.ctx = lax.axis_size(CTX)

    def part(self, k):
        return pl.ds(k * self.rows, self.rows)

    def near_copy(self, which, k):
        return send(
            self.piece(2 * which + 1, k),
            self.near.at[which, self.part(k)],
            self.near_sem.at[0, which, k],
            self.near_sem.at[1, which, k],
            FSDP,
            flip(self.me, 1),
        )

    def far_copy(self, k):
        return send(
            self.piece(2, k),
            self.far.at[self.part(k)],
            self.far_sem.at[0, k],
            self.far_sem.at[1, k],
            FSDP,
            flip(self.me, 2),
        )

    def last_copy(self, other, k):
        return send(
            self.piece(0, k),
            self.last.at[self.place, self.part(k)],
            self.last_sem.at[0, other - 1, k],
            self.last_sem.at[1, other - 1, k],
            CTX,
            lax.rem(self.place + other, self.ctx),
        )

    def own_copy(self, k):
        return pltpu.make_async_copy(
            self.piece(0, k), self.last.at[self.place, self.part(k)], self.local.at[2 + k]
        )

    def start(self, which):
        for k in range(self.chunks):
            self.near_copy(which, k).start()

    def load(self, source, index):
        copy = pltpu.make_async_copy(source, self.stages[index], self.local.at[index])
        copy.start()
        return copy

    def add(self, r, k, index):
        step = 32 if self.rows % 32 == 0 else 16
        piece, stage = self.piece(r, k), self.stages[index]

        @tiles(self.rows, step)
        def _(at):
            here = pl.ds(at, step)
            total = piece[here].astype(WIDE) + stage[here].astype(WIDE)
            piece[here] = total.astype(LOW)

    def first(self, k):
        for which in range(2):
            self.near_copy(which, k).wait_recv()
        copies = [self.load(self.near.at[which, self.part(k)], which) for which in range(2)]
        copies[1].wait()
        self.add(2, k, 1)
        self.far_copy(k).start()
        copies[0].wait()
        self.add(0, k, 0)

    def second(self, k):
        self.far_copy(k).wait_recv()
        self.load(self.far.at[self.part(k)], 0).wait()
        self.add(0, k, 0)
        for other in range(1, self.ctx):
            self.last_copy(other, k).start()
        self.own_copy(k).start()

    def finish(self):
        for k in range(self.chunks):
            for other in range(1, self.ctx):
                self.last_copy(other, k).wait_recv()
                self.last_copy(other, k).wait_send()
            self.own_copy(k).wait()
            self.far_copy(k).wait_send()
            for which in range(2):
                self.near_copy(which, k).wait_send()

    @staticmethod
    def sems(chunks):
        ctx = lax.axis_size(CTX)
        shapes = ((2, 2, chunks), (2, chunks), (2, ctx - 1, chunks), (2 + chunks,))
        return tuple(pltpu.SemaphoreType.DMA(shape) for shape in shapes)


class RowSum:
    def __init__(self, rows, came, sems, axes):
        self.rows, self.came, self.sems = rows, came, sems
        self.hops = [(axis, bit) for axis in axes for bit in bits_of(axis)]

    def copy(self, n):
        axis, bit = self.hops[n]
        return send(
            self.rows,
            self.came.at[n],
            self.sems.at[0, n],
            self.sems.at[1, n],
            axis,
            flip(lax.axis_index(axis), bit),
        )

    def start(self, n):
        if n < len(self.hops):
            self.copy(n).start()

    def move(self, n):
        if n < len(self.hops):
            self.copy(n).wait()
            self.rows[...] += self.came[n]
            self.start(n + 1)


def line_sems(tokens):
    rows, chunks = split_rows(tokens)
    return tuple(pltpu.SemaphoreType.DMA((2, chunks)) for _ in range(2))


def call_kernel(body, ident, far, near, scalars, far_outs, near_outs, scratch):
    groups = (far, near, scalars)
    spaces = (pl.ANY, pltpu.VMEM, pltpu.SMEM)
    arrays, in_specs = [], []
    for group, space in zip(groups, spaces):
        arrays += list(group.values())
        in_specs += [pl.BlockSpec(memory_space=space)] * len(group)
    outs = dict(far_outs, **near_outs)
    out_specs = [pl.BlockSpec(memory_space=pl.ANY)] * len(far_outs)
    out_specs += [pl.BlockSpec(memory_space=pltpu.VMEM)] * len(near_outs)
    shapes, tree = jax.tree.flatten(scratch)
    ins = [name for group in groups for name in group]

    def kernel(*refs):
        held = dict(zip(ins + list(outs), refs))
        held.update(jax.tree.unflatten(tree, refs[len(ins) + len(outs) :]))
        body(types.SimpleNamespace(**held))

    given = pl.pallas_call(
        kernel,
        out_shape=[jax.ShapeDtypeStruct(shape, kind) for shape, kind in outs.values()],
        in_specs=in_specs,
        out_specs=out_specs,
        scratch_shapes=shapes,
        compiler_params=pltpu.CompilerParams(
            collective_id=ident, has_side_effects=True, vmem_limit_bytes=VMEM_BYTES
        ),
    )(*arrays)
    return dict(zip(outs, given))


def front_body(r):
    me, place, zone = lax.axis_index(FSDP), lax.axis_index(CTX), lax.axis_index(TP)
    fsdp, ctx, tp = lax.axis_size(FSDP), lax.axis_size(CTX), lax.axis_size(TP)
    tokens, width = r.stream_hbm.shape
    columns = width // fsdp
    query_width = r.query.shape[1]
    heads = query_width // HD
    inner = r.up_shard.shape[1]
    length = r.lengths[0]
    line = Line(tokens)
    step_rows, chunks = line.rows, line.chunks

    ready = greet(all_peers())
    stream_load = pltpu.make_async_copy(r.stream_hbm, r.stream, r.load_sem.at[0])
    stream_load.start()

    def block_rows(held):
        size = held.shape[0] // fsdp

        def view(block, rows):
            start = pl.multiple_of(block * size + rows.start, 16)
            return held.at[pl.ds(start, rows.size)]

        return view

    gathers = types.SimpleNamespace(
        query=Gather(r.query_shard, block_rows(r.query), r.query_sems, 1),
        pair=Gather(r.pair_shard, block_rows(r.pair), r.pair_sems, 1),
        output=Gather(r.output_shard, lambda b, rows: r.output.at[b, rows], r.output_sems, 1),
        up=Gather(r.up_shard, block_rows(r.up_all), r.up_sems, r.up_sems[1].shape[1]),
        down=Gather(
            r.down_shard, lambda b, rows: r.down_all.at[b, rows], r.down_sems, r.down_sems[1].shape[1]
        ),
    )

    def small_copy(k):
        target = flip(me, k) if k < 3 else flip(flip(me, 1), 2)
        return send(
            r.smalls.at[0], r.smalls.at[k], r.small_sem.at[0, k - 1], r.small_sem.at[1, k - 1],
            FSDP, target,
        )

    r.smalls[0] = r.packed[...]
    ready()
    for k in range(1, fsdp):
        small_copy(k).start()
    gathers.pair.start()
    gathers.query.start()
    for k in range(1, fsdp):
        small_copy(k).wait()
    query_add = jnp.zeros((1, query_width), WIDE)
    value_add = jnp.zeros((1, HD), WIDE)
    for k in range(fsdp):
        block = me if k == 0 else flip(me, k) if k < 3 else flip(flip(me, 1), 2)
        at = pl.ds(pl.multiple_of(block * columns, columns), columns)
        r.vectors[pl.ds(0, 6), at] = r.smalls[k, pl.ds(0, 6), :]
        query_add += r.smalls[k, pl.ds(6, 1), pl.ds(0, query_width)]
        value_add += r.smalls[k, pl.ds(7, 1), pl.ds(0, HD)]
    for q in range(inner // columns):
        total = jnp.zeros((1, columns), WIDE)
        for k in range(fsdp):
            total += r.smalls[k, pl.ds(8 + q, 1), :]
        r.vectors[pl.ds(6, 1), pl.ds(q * columns, columns)] = total
    r.vectors[pl.ds(7, 1), :] = jnp.zeros((1, r.vectors.shape[1]), WIDE)

    def vector(n):
        return r.vectors[pl.ds(n, 1), pl.ds(0, width)]

    stream_load.wait()
    norm_step = min(32, tokens)

    @tiles(tokens, norm_step)
    def _(row):
        rows = pl.ds(row, norm_step)
        unit, scaled = norm_of(r.stream[rows, :].astype(WIDE))
        r.input_one[rows, :] = (unit * vector(0) + vector(1)).astype(LOW)

    early = (gathers.pair, gathers.query)
    for one in early:
        one.cross(0)
    for one in early:
        one.pass_on(0)
    for one in (gathers.output, gathers.up, gathers.down):
        one.start()
    gathers.pair.ready()
    own_rows = pl.ds(pl.multiple_of(place * tokens, tokens), tokens)
    key_half = mm(r.input_one[...], r.pair[...])
    r.pairs[own_rows, pl.ds(0, HD)] = key_half[:, :HD].astype(LOW)
    r.pairs[own_rows, pl.ds(HD, HD)] = (key_half[:, HD:] + value_add).astype(LOW)

    def pair_copy(other):
        return send(
            r.pairs.at[own_rows],
            r.pairs.at[own_rows],
            r.exchange_sem.at[0, other - 1],
            r.exchange_sem.at[1, other - 1],
            CTX,
            lax.rem(place + other, ctx),
        )

    for other in range(1, ctx):
        pair_copy(other).start()
    gathers.query.ready()
    r.queries[...] = (mm(r.input_one[...], r.query[...]) + query_add).astype(LOW)
    gathers.output.cross(0)
    for other in range(1, ctx):
        pair_copy(other).wait_recv()
    gathers.output.pass_on(0)

    share = 4 * step_rows
    factor = 1.0 / math.sqrt(HD)

    def attend(start):
        rows = pl.ds(start, share)
        keys = r.pairs[:, pl.ds(0, HD)]
        values = r.pairs[:, pl.ds(HD, HD)]
        shape = (share, keys.shape[0])
        query_at = place * tokens + start + lax.broadcasted_iota(jnp.int32, shape, 0)
        key_at = lax.broadcasted_iota(jnp.int32, shape, 1)
        allowed = (key_at <= query_at) & (key_at < length)
        for head in range(heads):
            at = pl.ds(head * HD, HD)
            scores = jnp.where(allowed, mm_nt(r.queries[rows, at], keys) * factor, NEGATIVE)
            peak = jnp.max(scores, -1, keepdims=True)
            soft = jnp.exp(scores - peak)
            total = jnp.sum(soft, -1, keepdims=True)
            r.mixture[rows, at] = mm((soft / total).astype(LOW), values).astype(LOW)
            r.log_total[rows, pl.ds(head, 1)] = peak + jnp.log(total)

    def project(start):
        rows = pl.ds(start, share)
        for block in range(fsdp):
            at = pl.ds(block * columns, columns)
            r.sum_own[rows, at] = mm(r.mixture[rows, :], r.output[block]).astype(LOW)

    branch_sum = LineSum(r.sum_own, r.sum_slots, r.sum_sems)
    spread = LineSpread(r.input_two, r.spread_sems)
    r.squares[...] = jnp.zeros_like(r.squares)

    def home(half, k):
        branch = branch_sum.total(half, k) + vector(2)
        middle = r.stream[line.at(half, k), :].astype(WIDE) + branch
        r.middle[pl.ds(k * step_rows, step_rows), :] = middle
        unit, scaled = norm_of(middle)
        r.input_two[line.at(half, k), :] = (unit * vector(3) + vector(4)).astype(LOW)
        spread.begin(half, k)
        slot = place * tokens + half * line.half + k * step_rows
        slots = slot + lax.broadcasted_iota(jnp.int32, (step_rows, width), 0)
        keep = jnp.where(slots < length, 1.0, 0.0)
        r.squares[...] += jnp.sum(keep * branch * branch, 0, keepdims=True)

    big = [(gathers.up, k) for k in range(gathers.up.cut)]
    big += [(gathers.down, k) for k in range(gathers.down.cut)]
    events = []
    for index, (one, k) in enumerate(big):
        events.append(functools.partial(one.cross, k))
        if index > 0:
            before, last = big[index - 1]
            events.append(functools.partial(before.pass_on, last))
    events.append(functools.partial(big[-1][0].pass_on, big[-1][1]))

    def move_on(count):
        for event in events[:count]:
            event()
        del events[:count]

    flow = Flow(branch_sum, spread, home, 1)
    groups = line.half // share
    for group in range(groups):
        for half in range(2):
            start = half * line.half + group * share
            attend(start)
            if group == 0 and half == 0:
                gathers.output.ready()
            project(start)
        flow.launch(4 * group, 4 * group + 4)
        if group < groups - 1:
            flow.advance(1)
            move_on(1)
    while flow.now < flow.steps:
        flow.advance(1)
        move_on(1)
    move_on(len(events))
    keeps = [
        pltpu.make_async_copy(source, target, r.load_sem.at[1 + n])
        for n, (source, target) in enumerate(
            ((r.query, r.query_all), (r.pair, r.pair_all), (r.output, r.output_all))
        )
    ]
    for copy in keeps:
        copy.start()
    for one in (gathers.up, gathers.down):
        one.ready()
    for copy in keeps:
        copy.wait()
    for other in range(1, ctx):
        pair_copy(other).wait_send()
    for one in vars(gathers).values():
        one.drain()
    branch_sum.drain()
    spread.drain()


def front(values, tokens):
    fsdp, ctx = lax.axis_size(FSDP), lax.axis_size(CTX)
    stream = values.stream
    width = stream.shape[1]
    columns = width // fsdp
    inner = values.up.shape[1]
    query_width = values.query.shape[1]
    pair_width = 2 * HD
    dma = pltpu.SemaphoreType.DMA
    wide_row = max(width, inner)
    return call_kernel(
        front_body,
        1,
        dict(stream_hbm=stream),
        dict(
            packed=values.packed,
            query_shard=values.query,
            pair_shard=values.pair,
            output_shard=values.output,
            up_shard=values.up,
            down_shard=values.down,
        ),
        dict(lengths=values.lengths),
        dict(
            up_all=((width, inner), LOW),
            down_all=((fsdp, inner, columns), LOW),
            query_all=((width, query_width), LOW),
            pair_all=((width, pair_width), LOW),
            output_all=((fsdp, query_width, columns), LOW),
        ),
        dict(
            vectors=((8, wide_row), WIDE),
            input_one=((tokens, width), LOW),
            input_two=((tokens, width), LOW),
            queries=((tokens, query_width), LOW),
            pairs=((tokens * ctx, pair_width), LOW),
            mixture=((tokens, query_width), LOW),
            log_total=((tokens, query_width // HD), WIDE),
            middle=((tokens // 2, width), WIDE),
            squares=((1, width), WIDE),
        ),
        dict(
            stream=pltpu.VMEM((tokens, width), LOW),
            smalls=pltpu.VMEM((fsdp,) + values.packed.shape, WIDE),
            query=pltpu.VMEM((width, query_width), LOW),
            pair=pltpu.VMEM((width, pair_width), LOW),
            output=pltpu.VMEM((fsdp, query_width, columns), LOW),
            sum_own=pltpu.VMEM((tokens, width), LOW),
            sum_slots=pltpu.VMEM((tokens, width), LOW),
            sum_sems=line_sems(tokens),
            spread_sems=line_sems(tokens),
            query_sems=Gather.sems(1),
            pair_sems=Gather.sems(1),
            output_sems=Gather.sems(1),
            up_sems=Gather.sems(2),
            down_sems=Gather.sems(2),
            load_sem=dma((4,)),
            small_sem=dma((2, fsdp - 1)),
            exchange_sem=dma((2, ctx - 1)),
        ),
    )


def back_body(r):
    me, place, zone = lax.axis_index(FSDP), lax.axis_index(CTX), lax.axis_index(TP)
    fsdp, ctx, tp = lax.axis_size(FSDP), lax.axis_size(CTX), lax.axis_size(TP)
    tokens, width = r.input_two_hbm.shape
    inner = r.up_hbm.shape[1]
    columns = width // fsdp
    share = tokens // tp
    query_width = r.queries_hbm.shape[1]
    heads = query_width // HD
    length = r.lengths[0]
    line = Line(tokens)
    step_rows, chunks = line.rows, line.chunks
    step = columns
    blocks = inner // step

    ready = greet(all_peers())

    def up_load(q):
        at = pl.ds(q, step)
        return pltpu.make_async_copy(r.up_hbm.at[:, at], r.up.at[:, at], r.weight_sem.at[0, q // step])

    def down_load(q):
        at = pl.ds(q, step)
        return pltpu.make_async_copy(
            r.down_hbm.at[:, at], r.down.at[:, at], r.weight_sem.at[1, q // step]
        )

    at_end = jnp.where(zone == tp - 1, tokens // 2, 0)
    pairs_of = dict(
        input_two=(r.input_two_hbm, r.input_two),
        cotangent=(r.cotangent_hbm, r.grad_feed),
        output=(r.output_hbm, r.output),
        queries=(r.queries_hbm, r.queries),
        pairs=(r.pairs_hbm, r.pairs),
        mixture=(r.mixture_hbm, r.mixture),
        query=(r.query_hbm, r.query),
        pair=(r.pair_hbm, r.pair),
        middle=(r.middle_hbm, r.middle),
        stream=(r.stream_hbm.at[pl.ds(pl.multiple_of(at_end, tokens // 2), tokens // 2)], r.stream),
    )
    loads = {}
    for index, (name, (source, target)) in enumerate(pairs_of.items()):
        loads[name] = pltpu.make_async_copy(source, target, r.load_sem.at[index])
    loads = types.SimpleNamespace(**loads)
    loads.input_two.start()
    loads.cotangent.start()
    for q in range(blocks):
        up_load(q * step).start()
        down_load(q * step).start()
    for name, copy in vars(loads).items():
        if copy is not loads.input_two and copy is not loads.cotangent:
            copy.start()
    r.rows[...] = jnp.zeros_like(r.rows)
    loads.cotangent.wait()

    @tiles(tokens, step_rows)
    def _(row):
        rows = pl.ds(row, step_rows)
        slots = place * tokens + row + lax.broadcasted_iota(jnp.int32, (step_rows, width), 0)
        keep = jnp.where(slots < length, 1.0, 0.0)
        r.grad_feed[rows, :] = (keep * r.grad_feed[rows, :].astype(WIDE)).astype(LOW)

    loads.input_two.wait()

    def vector(n):
        return r.vectors[pl.ds(n, 1), pl.ds(0, width)]

    def note(row, values):
        r.rows[pl.ds(row, 1), pl.ds(0, width)] += jnp.sum(values, 0, keepdims=True)

    @tiles(inner, step)
    def _(q):
        up_load(q).wait()
        down_load(q).wait()
        at = pl.ds(q, step)
        r.work_one[...] = mm(r.input_two[...], r.up[:, at])
        total = mm_nt(r.grad_feed[:, pl.ds(0, columns)], r.down[0, at, :])
        for block in range(1, fsdp):
            total += mm_nt(r.grad_feed[:, pl.ds(block * columns, columns)], r.down[block, at, :])
        r.work_two[...] = total
        bias = r.vectors[pl.ds(6, 1), at]

        @tiles(tokens, 32)
        def _(row):
            here = pl.ds(row, 32)
            v = r.work_one[here, :] + bias
            square = v * v
            reach = math.sqrt(2.0 / math.pi)
            t = jnp.tanh(reach * v * (1.0 + 0.044715 * square))
            gate = 0.5 * (1.0 + t)
            slope = gate + 0.5 * v * (1.0 - t * t) * reach * (1.0 + 3 * 0.044715 * square)
            r.hidden[here, at] = (v * gate).astype(LOW)
            grad = (r.work_two[here, :] * slope).astype(LOW)
            r.grad_pre[here, at] = grad
            r.rows[pl.ds(9, 1), at] += jnp.sum(grad.astype(WIDE), 0, keepdims=True)

    ready()
    sum_two = LineSum(r.sum_own, r.sum_slots, r.two_sems)
    sum_feed = LineSum(r.feed_own, r.feed_slots, r.feed_sems)
    sum_one = LineSum(r.sum_own, r.sum_slots, r.one_sems)
    spread_branch = LineSpread(r.grad_branch, r.branch_sems)
    spread_result = LineSpread(r.result, r.result_sems)
    spread_stream = LineSpread(r.stream_grad, r.stream_sems)

    @tiles(width, step)
    def _(col):
        at = pl.ds(col, step)
        r.sum_own[:, at] = mm_nt(r.grad_pre[...], r.up[at, :]).astype(LOW)

    for half in range(2):
        sum_two.launch(half)

    def turn(n):
        target = me
        for bit in (1, 2):
            if n & bit:
                target = flip(target, bit)
        return pl.ds(pl.multiple_of(target * columns, columns), columns)

    up_chunks, down_chunks = r.up_sems[1].shape[1], r.down_sems[1].shape[1]
    up_rows, down_rows = columns // up_chunks, inner // down_chunks

    def whole_piece(held, kept, size):
        if held is not None:
            return lambda n, k: held.at[n]
        return lambda n, k: kept.at[:, pl.ds(n * size, size)]

    def stage_part(rows, size):
        return [r.stage_down.at[n, pl.ds(0, rows), pl.ds(0, size)] for n in range(2)]

    sums = types.SimpleNamespace(
        up=PieceSum(
            lambda n, k: r.up.at[pl.ds(n * columns + k * up_rows, up_rows)],
            r.up_near,
            r.up_far,
            r.up_last,
            [r.stage_up.at[n] for n in range(2)],
            r.up_sems,
            up_chunks,
        ),
        down=PieceSum(
            lambda n, k: r.down.at[n, pl.ds(k * down_rows, down_rows)],
            r.down_near,
            r.down_far,
            r.down_last,
            [r.stage_down.at[n] for n in range(2)],
            r.down_sems,
            down_chunks,
        ),
        output=PieceSum(
            whole_piece(getattr(r, "output_piece", None), r.grad_pre, columns),
            r.output_near,
            r.output_far,
            r.output_last,
            stage_part(query_width, columns),
            r.output_sems,
            1,
        ),
        query=PieceSum(
            whole_piece(getattr(r, "query_piece", None), r.hidden, query_width),
            r.query_near,
            r.query_far,
            r.query_last,
            stage_part(columns, query_width),
            r.query_sems,
            1,
        ),
        pair=PieceSum(
            lambda n, k: r.pair_piece.at[n],
            r.pair_near,
            r.pair_far,
            r.pair_last,
            stage_part(columns, 2 * HD),
            r.pair_sems,
            1,
        ),
    )

    def up_terms(n):
        left = r.input_two[:, turn(n)]

        @tiles(inner, step)
        def _(q):
            part = mm_tn(left, r.grad_pre[:, pl.ds(q, step)])
            r.up[pl.ds(n * columns, columns), pl.ds(q, step)] = part.astype(LOW)

    def down_terms(n):
        right = r.grad_feed[:, turn(n)]

        @tiles(inner, step)
        def _(q):
            r.down[n, pl.ds(q, step), :] = mm_tn(r.hidden[:, pl.ds(q, step)], right).astype(LOW)

    def feed_terms(block):
        at = pl.ds(block * columns, columns)
        r.feed_own[:, at] = mm(r.hidden[...], r.down[block]).astype(LOW)

    def home_two(half, k):
        rows = line.at(half, k)
        unit, scaled = norm_of(r.middle[pl.ds(k * step_rows, step_rows), :])
        upstream = sum_two.total(half, k)
        note(0, upstream * unit)
        note(1, upstream)
        own = r.grad_feed[rows, :].astype(WIDE)
        note(3, own)
        grad = own + norm_backward(upstream, unit, scaled, vector(3))
        r.grad_middle[pl.ds(k * step_rows, step_rows), :] = grad
        rounded = grad.astype(LOW)
        note(2, rounded.astype(WIDE))
        r.grad_branch[rows, :] = rounded
        spread_branch.begin(half, k)

    tasks, late = [], []

    def first(one, k):
        one.first(k)
        late.append((one, k))

    def plan(work, *given):
        tasks.append(functools.partial(work, *given))

    def work_on(count):
        for task in tasks[:count]:
            task()
        del tasks[:count]

    plan(up_terms, 1)
    plan(sums.up.start, 0)
    plan(up_terms, 3)
    plan(sums.up.start, 1)
    plan(up_terms, 2)
    plan(up_terms, 0)
    for k in range(up_chunks):
        plan(first, sums.up, k)
    for block in range(fsdp):
        plan(feed_terms, block)
    plan(down_terms, 1)
    plan(sums.down.start, 0)
    plan(down_terms, 3)
    plan(sums.down.start, 1)
    plan(down_terms, 2)
    plan(down_terms, 0)
    for k in range(down_chunks):
        plan(first, sums.down, k)

    loads.middle.wait()
    work_on(4)
    for copy in (loads.output, loads.queries, loads.pairs, loads.mixture):
        copy.wait()
    r.grad_pairs[...] = jnp.zeros_like(r.grad_pairs)

    def home_feed(half, k):
        rows = line.at(half, k)
        feed = sum_feed.total(half, k) + vector(5)
        total = r.middle[pl.ds(k * step_rows, step_rows), :] + feed
        slot = place * tokens + half * line.half + k * step_rows
        slots = slot + lax.broadcasted_iota(jnp.int32, (step_rows, width), 0)
        keep = jnp.where(slots < length, 1.0, 0.0)
        note(6, keep * total * total)
        note(7, keep * feed * feed)
        r.feed_own[rows, :] = (keep * total).astype(LOW)
        spread_result.begin(half, k, r.feed_own)

    def attend_share(start):
        rows = pl.ds(start, share)
        total = mm_nt(r.grad_branch[rows, pl.ds(0, columns)], r.output[0])
        for block in range(1, fsdp):
            total += mm_nt(r.grad_branch[rows, pl.ds(block * columns, columns)], r.output[block])
        r.grad_mixture[...] = total.astype(LOW)
        keys = r.pairs[:, pl.ds(0, HD)]
        values = r.pairs[:, pl.ds(HD, HD)]
        shape = (share, keys.shape[0])
        query_at = place * tokens + start + lax.broadcasted_iota(jnp.int32, shape, 0)
        key_at = lax.broadcasted_iota(jnp.int32, shape, 1)
        allowed = (key_at <= query_at) & (key_at < length)
        factor = 1.0 / math.sqrt(HD)
        for head in range(heads):
            at = pl.ds(head * HD, HD)
            query = r.queries[rows, at]
            grad_mix = r.grad_mixture[:, at]
            scores = jnp.where(allowed, mm_nt(query, keys) * factor, NEGATIVE)
            soft = jnp.exp(scores - r.log_total[rows, pl.ds(head, 1)])
            grad_soft = mm_nt(grad_mix, values)
            dot_rows = jnp.sum(soft * grad_soft, -1, keepdims=True)
            grad_scores = (soft * (grad_soft - dot_rows) * factor).astype(LOW)
            r.grad_queries[rows, at] = mm(grad_scores, keys).astype(LOW)
            r.grad_pairs[:, pl.ds(0, HD)] += mm_tn(grad_scores, query)
            r.grad_pairs[:, pl.ds(HD, HD)] += mm_tn(soft.astype(LOW), grad_mix)

    def move_on(count):
        for one, k in late[:count]:
            one.second(k)
        del late[:count]

    flow_two = Flow(sum_two, spread_branch, home_two, 1)
    flow_feed = Flow(sum_feed, spread_result, home_feed, 1)
    starts = [half * line.half + group * share for group in range(tp // 2) for half in range(2)]
    per_share = share // step_rows
    while flow_two.now < flow_two.steps:
        flow_two.advance(1)
        work_on(2)
        if flow_two.now > 2:
            move_on(1)
        group = tp // 2 - (len(starts) + 1) // 2
        if starts and flow_two.now > flow_two.ready((group + 1) * per_share - 1):
            attend_share(starts.pop(0))
    work_on(len(tasks))
    flow_feed.launch()
    for start in starts:
        attend_share(start)
        flow_feed.advance(1)
    loads.query.wait()
    loads.pair.wait()

    def pair_out(other):
        target = lax.rem(place + other, ctx)
        rows = pl.ds(pl.multiple_of(target * tokens, tokens), tokens)
        r.pair_sent[other - 1] = r.grad_pairs[rows, :].astype(LOW)
        return send(
            r.pair_sent.at[other - 1],
            r.pair_came.at[other - 1],
            r.pair_ctx_sem.at[0, other - 1],
            r.pair_ctx_sem.at[1, other - 1],
            CTX,
            target,
        )

    ctx_copies = [pair_out(other) for other in range(1, ctx)]
    for copy in ctx_copies:
        copy.start()
    sum_two.drain()

    @tiles(width, step)
    def _(col):
        at = pl.ds(col, step)
        r.sum_own[:, at] = mm_nt(r.grad_queries[...], r.query[at, :]).astype(LOW)

    flow_one = Flow(sum_one, spread_stream, lambda half, k: home_one(half, k), 1)
    flow_one.launch()
    for copy in ctx_copies:
        copy.wait()
    own_rows = pl.ds(pl.multiple_of(place * tokens, tokens), tokens)
    own_pairs = r.grad_pairs[own_rows, :]
    for other in range(1, ctx):
        own_pairs += r.pair_came[other - 1].astype(WIDE)
    r.pair_own[...] = own_pairs.astype(LOW).reshape(r.pair_own.shape)

    def pair_line(other):
        target = lax.rem(zone + other, tp)
        return send(
            r.pair_own.at[target],
            r.pair_terms.at[other - 1],
            r.pair_line_sem.at[0, other - 1],
            r.pair_line_sem.at[1, other - 1],
            TP,
            target,
        )

    def pair_spread(other):
        return send(
            r.pair_all.at[zone],
            r.pair_all.at[zone],
            r.pair_line_sem.at[2, other - 1],
            r.pair_line_sem.at[3, other - 1],
            TP,
            lax.rem(zone + other, tp),
        )

    for other in range(1, tp):
        pair_line(other).start()

    r.rows[pl.ds(10, 1), pl.ds(0, query_width)] = jnp.sum(
        r.grad_queries[...].astype(WIDE), 0, keepdims=True
    )
    loads_one = pltpu.make_async_copy(r.input_one_hbm, r.input_two, r.load_sem.at[0])
    loads_one.start()

    def output_terms(n):
        terms = mm_tn(r.mixture[...], r.grad_branch[:, turn(n)])
        sums.output.piece(n, 0)[...] = terms.astype(LOW)

    def query_terms(n):
        terms = mm_tn(r.input_two[:, turn(n)], r.grad_queries[...])
        sums.query.piece(n, 0)[...] = terms.astype(LOW)

    def pair_terms(n):
        terms = mm_tn(r.input_two[:, turn(n)], r.pair_all[...].reshape(tokens, 2 * HD))
        r.pair_piece[n] = terms.astype(LOW)

    def begin(one, terms):
        plan(terms, 1)
        plan(one.start, 0)
        plan(terms, 3)
        plan(one.start, 1)
        plan(terms, 2)
        plan(terms, 0)

    def pair_shares():
        total = r.pair_own[zone].astype(WIDE)
        for other in range(1, tp):
            pair_line(other).wait_recv()
            total += r.pair_terms[other - 1].astype(WIDE)
        r.pair_all[zone] = total.astype(LOW)
        for other in range(1, tp):
            pair_spread(other).start()

    def pair_gathered():
        for other in range(1, tp):
            pair_spread(other).wait_recv()
        values = r.pair_all[...].reshape(tokens, 2 * HD)[:, HD:]
        r.rows[pl.ds(11, 1), pl.ds(0, HD)] = jnp.sum(values.astype(WIDE), 0, keepdims=True)

    def home_one(half, k):
        rows = line.at(half, k)
        here = pl.ds(k * step_rows, step_rows)
        unit, scaled = norm_of(r.stream[here, :].astype(WIDE))
        at = half * line.half + k * step_rows
        pair_rows = r.pair_all[at // share, pl.ds(at % share, step_rows), :]
        upstream = sum_one.total(half, k) + mm_nt(pair_rows, r.pair[...])
        note(4, upstream * unit)
        note(5, upstream)
        grad = r.grad_middle[here, :] + norm_backward(upstream, unit, scaled, vector(0))
        r.sum_own[rows, :] = grad.astype(LOW)
        spread_stream.begin(half, k, r.sum_own)

    begin(sums.output, output_terms)
    plan(loads_one.wait)
    begin(sums.query, query_terms)
    plan(first, sums.output, 0)
    plan(first, sums.query, 0)
    begin(sums.pair, pair_terms)
    plan(first, sums.pair, 0)
    loads.stream.wait()
    work_on(3)
    pair_shares()
    work_on(4)
    pair_gathered()
    while flow_one.now < flow_one.steps:
        flow_one.advance(1)
        work_on(3)
        flow_feed.advance(1)
        if flow_one.now % 3 == 2:
            move_on(1)
    work_on(len(tasks))
    flow_feed.advance(flow_feed.steps)
    move_on(len(late))

    for half in range(2):

        @pl.when(line.is_home(half))
        def _():
            rows = pl.ds(half * line.half, line.half)
            copies = [
                pltpu.make_async_copy(r.feed_own.at[rows], r.result.at[rows], r.keep_sem.at[0]),
                pltpu.make_async_copy(r.sum_own.at[rows], r.stream_grad.at[rows], r.keep_sem.at[1]),
            ]
            for copy in copies:
                copy.start()
            for copy in copies:
                copy.wait()

    for one in (sum_feed, sum_one, spread_branch, spread_result, spread_stream):
        one.drain()
    for other in range(1, tp):
        pair_line(other).wait_send()
        pair_spread(other).wait_send()
    for one in vars(sums).values():
        one.finish()


def back(values, front_given):
    fsdp, ctx, tp = lax.axis_size(FSDP), lax.axis_size(CTX), lax.axis_size(TP)
    g = types.SimpleNamespace(**front_given)
    tokens, width = g.input_two.shape
    inner = g.up_all.shape[1]
    columns = width // fsdp
    share = tokens // tp
    query_width = g.queries.shape[1]
    pair_width = 2 * HD
    key_count = g.pairs.shape[0]
    dma = pltpu.SemaphoreType.DMA
    far_outs = dict(
        result=((tokens, width), LOW),
        stream_grad=((tokens, width), LOW),
        up_last=((ctx, columns, inner), LOW),
        up_near=((2, columns, inner), LOW),
        up_far=((columns, inner), LOW),
        down_last=((ctx, inner, columns), LOW),
        down_near=((2, inner, columns), LOW),
        down_far=((inner, columns), LOW),
        output_last=((ctx, query_width, columns), LOW),
        output_near=((2, query_width, columns), LOW),
        output_far=((query_width, columns), LOW),
        query_last=((ctx, columns, query_width), LOW),
        query_near=((2, columns, query_width), LOW),
        query_far=((columns, query_width), LOW),
        pair_last=((ctx, columns, pair_width), LOW),
        pair_near=((2, columns, pair_width), LOW),
        pair_far=((columns, pair_width), LOW),
    )
    scratch = dict(
        up=pltpu.VMEM((width, inner), LOW),
        down=pltpu.VMEM((fsdp, inner, columns), LOW),
        input_two=pltpu.VMEM((tokens, width), LOW),
        grad_feed=pltpu.VMEM((tokens, width), LOW),
        hidden=pltpu.VMEM((tokens, inner), LOW),
        grad_pre=pltpu.VMEM((tokens, inner), LOW),
        work_one=pltpu.VMEM((tokens, columns), WIDE),
        work_two=pltpu.VMEM((tokens, columns), WIDE),
        sum_own=pltpu.VMEM((tokens, width), LOW),
        sum_slots=pltpu.VMEM((tokens, width), LOW),
        feed_own=pltpu.VMEM((tokens, width), LOW),
        feed_slots=pltpu.VMEM((tokens, width), LOW),
        grad_branch=pltpu.VMEM((tokens, width), LOW),
        middle=pltpu.VMEM((tokens // 2, width), WIDE),
        grad_middle=pltpu.VMEM((tokens // 2, width), WIDE),
        stream=pltpu.VMEM((tokens // 2, width), LOW),
        output=pltpu.VMEM((fsdp, query_width, columns), LOW),
        query=pltpu.VMEM((width, query_width), LOW),
        pair=pltpu.VMEM((width, pair_width), LOW),
        queries=pltpu.VMEM((tokens, query_width), LOW),
        pairs=pltpu.VMEM((key_count, pair_width), LOW),
        mixture=pltpu.VMEM((tokens, query_width), LOW),
        grad_mixture=pltpu.VMEM((share, query_width), LOW),
        grad_queries=pltpu.VMEM((tokens, query_width), LOW),
        grad_pairs=pltpu.VMEM((key_count, pair_width), WIDE),
        pair_sent=pltpu.VMEM((ctx - 1, tokens, pair_width), LOW),
        pair_came=pltpu.VMEM((ctx - 1, tokens, pair_width), LOW),
        pair_own=pltpu.VMEM((tp, share, pair_width), LOW),
        pair_terms=pltpu.VMEM((tp - 1, share, pair_width), LOW),
        pair_all=pltpu.VMEM((tp, share, pair_width), LOW),
        pair_piece=pltpu.VMEM((fsdp, columns, pair_width), LOW),
        stage_up=pltpu.VMEM((2, columns // 4, inner), LOW),
        stage_down=pltpu.VMEM((2, inner // 4, columns), LOW),
        weight_sem=dma((2, inner // columns)),
        load_sem=dma((10,)),
        keep_sem=dma((2,)),
        pair_ctx_sem=dma((2, ctx - 1)),
        pair_line_sem=dma((4, tp - 1)),
        two_sems=line_sems(tokens),
        feed_sems=line_sems(tokens),
        one_sems=line_sems(tokens),
        branch_sems=line_sems(tokens),
        result_sems=line_sems(tokens),
        stream_sems=line_sems(tokens),
        up_sems=PieceSum.sems(4),
        down_sems=PieceSum.sems(4),
        output_sems=PieceSum.sems(1),
        query_sems=PieceSum.sems(1),
        pair_sems=PieceSum.sems(1),
    )
    if tokens != query_width or inner < width:
        scratch.update(output_piece=pltpu.VMEM((fsdp, query_width, columns), LOW))
    if tokens != columns or inner < fsdp * query_width:
        scratch.update(query_piece=pltpu.VMEM((fsdp, columns, query_width), LOW))
    return call_kernel(
        back_body,
        2,
        dict(
            input_two_hbm=g.input_two,
            cotangent_hbm=values.cotangent,
            up_hbm=g.up_all,
            down_hbm=g.down_all,
            output_hbm=g.output_all,
            queries_hbm=g.queries,
            pairs_hbm=g.pairs,
            mixture_hbm=g.mixture,
            query_hbm=g.query_all,
            pair_hbm=g.pair_all,
            middle_hbm=g.middle,
            stream_hbm=values.stream,
            input_one_hbm=g.input_one,
        ),
        dict(vectors=g.vectors, log_total=g.log_total),
        dict(lengths=values.lengths),
        far_outs,
        dict(rows=((16, max(width, inner)), WIDE)),
        scratch,
    )


def swap(block, axis, bit):
    count = lax.axis_size(axis)
    return lax.ppermute(block, axis, [(place, place ^ bit) for place in range(count)])


def sum_over(values, axes):
    for axis in axes:
        for bit in bits_of(axis):
            values = values + swap(values, axis, bit)
    return values


def body(
    stream,
    cotangent,
    lengths,
    first_gain,
    first_shift,
    query_weight,
    query_bias,
    pair_weight,
    value_bias,
    output_weight,
    output_bias,
    second_gain,
    second_shift,
    up_weight,
    up_bias,
    down_weight,
    down_bias,
):
    fsdp = lax.axis_size(FSDP)
    me, place = lax.axis_index(FSDP), lax.axis_index(CTX)
    seq_count, group_len, width = stream.shape
    tokens = seq_count * group_len
    columns, inner = first_gain.shape[0], up_weight.shape[1]

    def placed(bias):
        spots = jnp.arange(fsdp)[None, :, None] == me
        return jnp.where(spots, bias.reshape(-1, 1, bias.shape[-1]).astype(WIDE), 0.0).reshape(-1)

    def row(values):
        return jnp.pad(values.astype(WIDE), (0, columns - values.shape[0]))[None]

    vectors = (first_gain, first_shift, output_bias, second_gain, second_shift, down_bias)
    packed = jnp.concatenate(
        [row(vector) for vector in vectors]
        + [row(placed(query_bias)), row(placed(value_bias.reshape(1, -1)))]
        + [placed(up_bias).reshape(-1, columns)]
    )
    packed = jnp.pad(packed, ((0, -packed.shape[0] % 8), (0, 0)))
    values = types.SimpleNamespace(
        stream=stream.reshape(tokens, width),
        cotangent=cotangent.reshape(tokens, width),
        lengths=lengths,
        packed=packed,
        query=query_weight,
        pair=pair_weight,
        output=output_weight,
        up=up_weight,
        down=down_weight,
    )
    given = front(values, tokens)
    ended = types.SimpleNamespace(**back(values, given))
    rows = ended.rows
    query_width = query_weight.shape[1]

    def finished(last):
        return jnp.sum(last.astype(WIDE), 0)

    held = place * tokens + jnp.arange(tokens) < lengths[0]
    end = jnp.where(lax.axis_index(TP) == 0, 1.0, 0.0)
    at_home = jnp.where(
        (lax.axis_index(TP) == 0) | (lax.axis_index(TP) == lax.axis_size(TP) - 1), 1.0, 0.0
    )
    shared = jnp.concatenate(
        [rows[k, :width] for k in range(6)]
        + [
            jnp.stack(
                [
                    jnp.sum(rows[6, :width]),
                    jnp.sum(given["squares"]) * at_home,
                    jnp.sum(rows[7, :width]),
                    jnp.sum(held.astype(WIDE)) * end,
                ]
            )
        ]
    )
    shared = sum_over(shared, (TP, FSDP, CTX))
    own = jnp.concatenate([rows[9, :inner], rows[10, :query_width], rows[11, :HD]])
    own = sum_over(own, (FSDP, CTX))
    up_bias_all = own[:inner].reshape(up_bias.shape[0], fsdp, -1)
    query_bias_all = own[inner : inner + query_width].reshape(query_bias.shape[0], fsdp, -1)

    def mine(row, size):
        return lax.dynamic_slice_in_dim(row, me * size, size, 0)

    totals = shared[6 * width :]
    root_means = jnp.sqrt(totals[:3] / (totals[3] * width))
    return (
        ended.result.reshape(stream.shape),
        ended.stream_grad.reshape(stream.shape),
        mine(shared[4 * width : 5 * width], columns),
        mine(shared[5 * width : 6 * width], columns),
        finished(ended.query_last),
        lax.dynamic_index_in_dim(query_bias_all, me, 1, False),
        finished(ended.pair_last),
        mine(own[inner + query_width :], value_bias.shape[0]),
        finished(ended.output_last),
        mine(shared[2 * width : 3 * width], columns),
        mine(shared[:width], columns),
        mine(shared[width : 2 * width], columns),
        finished(ended.up_last),
        lax.dynamic_index_in_dim(up_bias_all, me, 1, False),
        finished(ended.down_last),
        mine(shared[3 * width : 4 * width], columns),
        root_means,
    )


def solution(mesh):
    in_specs = (
        P(FSDP, CTX, None),
        P(FSDP, CTX, None),
        P(FSDP),
        P(FSDP),
        P(FSDP),
        P(FSDP, TP),
        P(TP, FSDP),
        P(FSDP, None),
        P(FSDP),
        P(TP, FSDP),
        P(FSDP),
        P(FSDP),
        P(FSDP),
        P(FSDP, TP),
        P(TP, FSDP),
        P(TP, FSDP),
        P(FSDP),
    )
    out_specs = (
        P(FSDP, CTX, None),
        P(FSDP, CTX, None),
        P(FSDP),
        P(FSDP),
        P(FSDP, TP),
        P(TP, FSDP),
        P(FSDP, None),
        P(FSDP),
        P(TP, FSDP),
        P(FSDP),
        P(FSDP),
        P(FSDP),
        P(FSDP, TP),
        P(TP, FSDP),
        P(TP, FSDP),
        P(FSDP),
        P(),
    )
    return jax.shard_map(body, mesh=mesh, in_specs=in_specs, out_specs=out_specs, check_vma=False)
```

time: 1550 us -> 481 us (0.31)
  waiting for transfers between devices: 1170 us -> 3.18 us
  Pallas kernels: 0 us -> 419 us
  blocking collectives: 160 us -> 0 us
  matrix products: 123 us -> 0 us
  local copies, waits for them, and re-layouts: 35.5 us -> 14.7 us
    psum x3 -> x0, waiting for transfers between devices: 570 us -> none  [the longest x1 286 us: body(): lax.psum(jnp.dot(hidden, down_full, preferred_element_type=jnp.float32),...]
    pallas_call x0 -> x2, Pallas kernels: none -> 419 us  [call_kernel(): pl.pallas_call(kernel, out_shape=[jax.ShapeDtypeStruct(shape, kind) for s...]
    reduce_scatter x6 -> x0, waiting for transfers between devices: 286 us -> none  [the longest x1 119 us: body(): lax.psum_scatter(weight_grads[10], ('fsdp', 'ctx'), scatter_dimension=0,...]
    all_gather x9 -> x0, waiting for transfers between devices: 244 us -> none  [the longest x1 58.3 us: body(): lax.all_gather(shares[10], 'ctx', axis=0, tiled=True)]
    dot_general x21 -> x0, matrix products: 123 us -> none  [the longest x1 14.7 us: body(): jnp.einsum('tf,td->fd', hidden, grad_feed, preferred_element_type=jnp.flo...]
    all_gather x18 -> x0, blocking collectives: 93.5 us -> none  [the longest x1 9.21 us: body(): lax.all_gather(key_values.reshape(seq_count, group_len, 2 * HD), 'ctx', a...]
    unnamed x22 -> x0, waiting for transfers between devices: 68.6 us -> none
    unnamed x3 -> x0, blocking collectives: 38 us -> none
  transfers between devices with their start and end apart: 20 -> 8, of which waited for: 15 -> 3; matrix products, arithmetic and copies ran while one was open for 7% -> 3% of each run, Pallas kernels for 0% -> 0%
where the time goes in v2:
time: 481 us; the launch traced here: 471 us
  Pallas kernels  419 us (87%)
  other arithmetic  20.4 us (4%)
  local copies, waits for them, and re-layouts  14.7 us (3%)
  starting transfers between devices  10 us (2%)
    pallas_call x2, Pallas kernels, call_kernel(): pl.pallas_call(kernel, out_shape=[jax.ShapeDtypeStruct(shape, kind) for s...  419 us
    reduce_sum x4, other arithmetic, finished(): return jnp.sum(last.astype(WIDE), 0)  11.1 us
    ppermute x8, starting transfers between devices, swap(): lax.ppermute(block, axis, [(place, place ^ bit) for place in range(count)])  10 us
  transfers between devices with their start and end apart: 8, of which 3 were waited for; matrix products, arithmetic and copies ran while one was open for 3% of the time, Pallas kernels for 0%

profile of v2, /device:TPU:0, one launch (start us, length us, event | category | flops | bytes accessed | tf_op | source)
XLA Modules:
  0.0 471.1 jit_solution(4711936563876717032)
XLA Ops:
  1.3 0.1 broadcast_in_dim.122
  1.4 0.1 broadcast_in_dim.123
  1.5 0.7 broadcast_in_dim.131
  2.2 0.7 broadcast_in_dim.132
  2.8 0.7 convert_element_type.40
  3.5 0.7 broadcast_in_dim.124
  4.2 0.1 broadcast_in_dim.125
  4.3 0.7 broadcast_in_dim.133
  5.0 0.7 broadcast_in_dim.134
  5.6 0.7 broadcast_in_dim.135
  6.3 0.7 broadcast_in_dim.136
  7.0 0.1 broadcast_select_fusion.1
  7.1 0.1 select_n.54
  7.2 0.7 convert_element_type.42
  7.8 0.1 broadcast_select_fusion
  7.9 0.1 select_n.57
  8.0 0.1 concatenate.9
  8.1 0.6 pad.9.refs_1_
  8.7 122.1 %shard_map.296 = (bf16[2048,2048]{1,0:T(8,128)(2,1)}, bf16[4,2048,512]{2,1,0:T(8,128)(2,1)}, bf16[2048,512]{1,0:T(8,128)(2,1)}, bf16[2048,256]{1,0:T(8,128)(2,1)...) custom-call(bf16[512,2048]{1,0:T(8,128)(2,1)} %bitcast.32, ...), custom_call_target="tpu_custom_call" | custom-call | tf_op jit(solution)/shard_map/pallas_call | solution.py:505
  130.8 296.9 %shard_map.297 = (bf16[512,2048]{1,0:T(8,128)(2,1)}, bf16[512,2048]{1,0:T(8,128)(2,1)}, bf16[2,512,2048]{2,1,0:T(8,128)(2,1)}, bf16[2,512,2048]{2,1,0:T(8,128)(2...) custom-call(bf16[512,2048]{1,0:T(8,128)(2,1)} %get-tuple-element.39., ...), custom_call_target="tpu_custom_call" | custom-call | tf_op jit(solution)/shard_map/pallas_call | solution.py:505
  427.7 0.7 slice_bitcast_fusion
  428.4 0.7 slice.100
  429.1 1.9 slice_reduce_fusion
  431.0 0.0 collective-permute-start.5
  431.0 0.0 copy-done.6
  431.1 0.6 reduce_sum.82
  431.7 0.6 convert_reduce_fusion.5
  433.6 1.4 concatenate.10
  435.0 0.0 collective-permute-start
  435.0 5.7 %convert_reduce_fusion.1 = f32[512,2048]{1,0:T(8,128)} fusion(bf16[2,512,2048]{2,1,0:T(8,128)(2,1)} %get-tuple-element.59), kind=kLoop, calls=%fused_computation.1 | loop fusion | flops 3145728 | bytes 8388608 | tf_op jit(solution)/shard_map/reduce_sum | solution.py:1433
  440.7 0.0 copy-done
  440.7 2.8 convert_reduce_fusion
  443.5 0.0 collective-permute-done.5
  443.5 0.1 collective-permute-start.6
  443.6 0.0 collective-permute-done
  443.6 3.7 collective-permute-start.1
  447.3 1.6 convert_reduce_fusion.2
  449.0 0.0 collective-permute-done.6
  449.0 2.1 collective-permute-start.7
  451.1 0.0 collective-permute-done.1
  451.1 0.1 collective-permute-start.2
  451.2 0.9 convert_reduce_fusion.4
  452.1 0.7 collective-permute-done.7
  452.8 0.1 slice.109
  452.9 0.0 collective-permute-done.2
  452.9 2.0 collective-permute-start.3
  454.9 0.6 constant_dynamic-slice_fusion
  455.5 0.1 slice.103
  455.6 1.5 collective-permute-done.3
  457.1 2.1 collective-permute-start.4
  459.2 0.6 constant_dynamic-slice_fusion.1
  459.8 0.6 dynamic_slice.32
  460.4 0.9 collective-permute-done.4
  461.3 0.6 slice.123
  462.6 0.5 fusion
  463.1 0.7 dynamic_slice.37
  463.7 0.7 dynamic_slice.35
  464.4 0.7 dynamic_slice.34
  465.0 0.7 dynamic_slice.33
  465.7 0.7 dynamic_slice.30
  466.4 0.7 dynamic_slice.29
  467.0 1.3 copy.37
  468.3 1.0 copy-done.1
  469.4 1.3 copy.38
  (27 shorter events, 0.1 us)
Async XLA Ops:
  130.8 300.3 %copy-start.6 = (f32[1,2048]{1,0:T(1,128)S(1)}, f32[1,2048]{1,0:T(1,128)}, u32[]{:S(2)}) copy-start(f32[1,2048]{1,0:T(1,128)} %get-tuple-element.55) | copy-start | bytes 24580
  431.0 12.5 %collective-permute-start.5 = (f32[2688]{0:T(1024)S(1)}, f32[2688]{0:T(1024)S(1)}, u32[]{:S(2)}, u32[]{:S(2)}) collective-permute-start(f32[2688]{0:T(1024)S(1)} %pad_maximum_fusion), channel_id=1, source_target_pairs={{0,8},{8,0},{16,24},{24,16},{1,9},{9,1},{17,25},{25,17},{2,10},{10... | collective-permute-start | bytes 32264 | tf_op jit(solution)/shard_map/ppermute | solution.py:1367
  435.0 8.7 %collective-permute-start = (f32[12292]{0:T(1024)S(1)}, f32[12292]{0:T(1024)S(1)}, u32[]{:S(2)}, u32[]{:S(2)}) collective-permute-start(f32[12292]{0:T(1024)S(1)} %concatenate.10), channel_id=1, source_target_pairs={{0,1},{1,0},{2,3},{3,2},{4,5},{5,4},{6,7},{7,6},{8,9},{9,8},{10,11... | collective-permute-start | bytes 147512 | tf_op jit(solution)/shard_map/ppermute | solution.py:1367
  435.0 5.7 %copy-start = (bf16[2,2048,512]{2,1,0:T(8,128)(2,1)S(1)}, bf16[2,2048,512]{2,1,0:T(8,128)(2,1)}, u32[]{:S(2)}) copy-start(bf16[2,2048,512]{2,1,0:T(8,128)(2,1)} %get-tuple-element.60) | copy-start | bytes 12582916
  440.7 6.6 %copy-start.3 = (bf16[2,512,512]{2,1,0:T(8,128)(2,1)S(1)}, bf16[2,512,512]{2,1,0:T(8,128)(2,1)}, u32[]{:S(2)}) copy-start(bf16[2,512,512]{2,1,0:T(8,128)(2,1)} %get-tuple-element.58) | copy-start | bytes 3145732
  440.7 6.6 %copy-start.4 = (bf16[2,512,512]{2,1,0:T(8,128)(2,1)S(1)}, bf16[2,512,512]{2,1,0:T(8,128)(2,1)}, u32[]{:S(2)}) copy-start(bf16[2,512,512]{2,1,0:T(8,128)(2,1)} %get-tuple-element.56) | copy-start | bytes 3145732
  443.5 5.5 %collective-permute-start.6 = (f32[2688]{0:T(1024)S(1)}, f32[2688]{0:T(1024)S(1)}, u32[]{:S(2)}, u32[]{:S(2)}) collective-permute-start(f32[2688]{0:T(1024)S(1)} %fusion.1), channel_id=1, source_target_pairs={{0,16},{8,24},{16,0},{24,8},{1,17},{9,25},{17,1},{25,9},{2,18},{10... | collective-permute-start | bytes 32264 | tf_op jit(solution)/shard_map/ppermute | solution.py:1367
  443.6 7.5 %collective-permute-start.1 = (f32[12292]{0:T(1024)S(1)}, f32[12292]{0:T(1024)S(1)}, u32[]{:S(2)}, u32[]{:S(2)}) collective-permute-start(f32[12292]{0:T(1024)S(1)} %add.53), channel_id=1, source_target_pairs={{0,2},{1,3},{2,0},{3,1},{4,6},{5,7},{6,4},{7,5},{8,10},{9,11},{10,... | collective-permute-start | bytes 147512 | tf_op jit(solution)/shard_map/ppermute | solution.py:1367
  447.3 3.9 copy-start.5
  447.3 19.7 %copy-start.2 = (bf16[512,2048]{1,0:T(8,128)(2,1)S(1)}, bf16[512,2048]{1,0:T(8,128)(2,1)}, u32[]{:S(2)}) copy-start(bf16[512,2048]{1,0:T(8,128)(2,1)} %get-tuple-element.52) | copy-start | bytes 6291460
  449.0 3.8 collective-permute-start.7
  451.1 1.8 collective-permute-start.2
  452.9 4.2 collective-permute-start.3
  457.1 4.2 collective-permute-start.4
  467.0 2.3 copy-start.1
